TPU v7x, 32 devices: a whole 2x2x4 slice. The times are simulated.
32 devices in a mesh: seq: 8 (over y, x, core), expert: 4 (over z).
Axes of the slice: x: 2, y: 2, z: 4, core: 2. Of those that a mesh axis runs over, the one named last changes fastest.
Arguments:
- layer_input: bfloat16 [512, 2, 4096], P(('seq', 'expert')), may hold values from -6 to 6
- x_branch: bfloat16 [512, 2, 4096], P('seq', None, 'expert'), may hold values from -24 to 24
- gate_branch: bfloat16 [512, 2, 4096], P('seq', None, 'expert'), may hold values from -6 to 6
- conv_weight: bfloat16 [4, 4096], P(None, 'expert'), may hold values from -3 to 3
- conv_bias: bfloat16 [4096], P('expert'), may hold values from -3 to 3
- x_proj: bfloat16 [4096, 288], P('expert'), may hold values from -0.09375 to 0.09375
- dt_proj: bfloat16 [256, 4096], P(None, 'expert'), may hold values from -0.375 to 0.375
- dt_bias: float32 [4096], P('expert'), may hold values from -5.5 to -2
- a_log: float32 [4096, 16], P('expert'), may hold values from -7 to 2.77
- d_skip: float32 [4096], P('expert'), may hold values from 0.5 to 1.5
- carry_state: float32 [2, 4096, 16], P(None, 'expert'), may hold values from -3 to 3
- carry_tail: bfloat16 [3, 2, 4096], P(None, None, 'expert'), may hold values from -6 to 6
- out_proj: bfloat16 [4096, 4096], P('expert'), may hold values from -0.09375 to 0.09375
- steering: bfloat16 [4096], replicated, may hold values from -6 to 6
- refusal: bfloat16 [4, 4096], replicated, may hold values from -6 to 6
- norm_gain: bfloat16 [4096], replicated, may hold values from 0.5 to 1.5
- router: bfloat16 [4096, 4], replicated, may hold values from -0.09375 to 0.09375
- specialist_switch_matrix: bfloat16 [4, 4096, 2048], P('expert', None, 'seq'), may hold values from -0.09375 to 0.09375
- w_up: bfloat16 [4, 4096, 2048], P('expert', None, 'seq'), may hold values from -0.09375 to 0.09375
- w_down: bfloat16 [4, 2048, 4096], P('expert', 'seq'), may hold values from -0.125 to 0.125
- expert_ids: int32 [512, 2, 2], P('seq'), may hold values from 0 to 3, all different within a row; in each aligned block of 128 rows (0 to 127, 128 to 255, ..., all dimensions but the last counted through in order) at most 80 rows name the same one
Outputs:
- layer_out: float32 [512, 2, 4096], P(('seq', 'expert'))
Inputs may be any that keep to these rules, and one draw needn't show every extreme that they name: `expert_ids`: in every aligned block of 128 rows in position-major order (the tokens of one seq index), no expert is named by more than 80 tokens, and in some block an expert is named by exactly 80; the two experts of a token differ.
All inputs are finite; a program needn't handle non-finite values.
Results may differ from a plain program's by a relative error of at most 0.0044.
Values may be sent and summed in bfloat16 or wider, within the bound.
A program may use at most 128 MiB of HBM per device.

v0:
```python
import jax
import jax.numpy as jnp
from jax import lax
from jax.experimental import pallas as pl
from jax.experimental.pallas import tpu as pltpu
from jax.sharding import PartitionSpec as P

EPS = 1e-06
VMEM_LIMIT = 48 * 1024 * 1024
LANES = 128


def passed_along(array, axis, by):
    count = lax.axis_size(axis)
    pairs = [(i, i + by) for i in range(count) if 0 <= i + by < count]
    return lax.ppermute(array, axis, pairs)


def remove_directions(steering, refusal):
    vector = steering.astype(jnp.float32)
    units = []
    for k in range(refusal.shape[0]):
        r = refusal[k].astype(jnp.float32)
        for q in units:
            r = r - jnp.sum(q * r) * q
        r = r * lax.rsqrt(jnp.sum(r * r) + EPS)
        units.append(r)
    for q in units:
        vector = vector - jnp.sum(q * vector) * q
    return vector


def root_mean_normed(residual, norm_gain):
    scaled = residual * lax.rsqrt(jnp.mean(residual * residual, axis=-1, keepdims=True) + EPS)
    return (scaled * norm_gain.astype(jnp.float32)).astype(jnp.bfloat16)


def owner_weight(normed, router, picked_indices, owner):
    experts = router.shape[1]
    logits = jnp.dot(normed, router, preferred_element_type=jnp.float32)
    labels = jnp.arange(experts, dtype=jnp.int32)
    onehot = (picked_indices[:, :, None] == labels[None, None, :]).astype(jnp.float32)
    picked = jnp.sum(onehot * logits[:, None, :], axis=-1)
    leading = jax.nn.sigmoid(picked[:, 0] - picked[:, 1])
    shares = jnp.stack([leading, 1.0 - leading], axis=1)
    per_expert = jnp.sum(onehot * shares[:, :, None], axis=1)
    return jnp.sum(per_expert * (labels == owner).astype(jnp.float32)[None, :], axis=1)


def slot_matrix(picked_indices, owner, capacity):
    member = jnp.any(picked_indices == owner, axis=1)
    order = jnp.cumsum(member.astype(jnp.int32)) - 1
    slots = jnp.arange(capacity, dtype=jnp.int32)
    return (order[None, :] == slots[:, None]) & member[None, :]


def state_kernel(length, prompts, nst, groups, low_ref, dtp_ref, dtb_ref, act_ref, alog_ref, b_ref,
                 dtx_ref, actx_ref, state_ref, total_ref):
    rows = length * prompts
    for k in range(groups):
        cols = pl.ds(k * LANES, LANES)
        raw = jnp.dot(low_ref[...], dtp_ref[:, cols], preferred_element_type=jnp.float32)
        dtx_ref[pl.ds(k, rows, stride=groups), :] = jax.nn.softplus(raw + dtb_ref[:, cols])
        actx_ref[pl.ds(k, rows, stride=groups), :] = act_ref[:, cols]
    rates = [-jnp.exp(alog_ref[n]) for n in range(nst)]
    for p in range(prompts):

        def step(t, carry):
            states, total = carry
            row = t * prompts + p
            at = pl.ds(pl.multiple_of(row * groups, groups), groups)
            dt = dtx_ref[at, :]
            drive = dt * actx_ref[at, :]
            states = tuple(
                jnp.exp(dt * rates[n]) * states[n] + drive * b_ref[row * 2 * nst + n]
                for n in range(nst)
            )
            return states, total + dt

        zero = jnp.zeros((groups, LANES), jnp.float32)
        states, total = lax.fori_loop(0, length, step, ((zero,) * nst, zero), unroll=4)
        for n in range(nst):
            state_ref[p, n] = states[n]
        total_ref[p] = total


def output_kernel(length, prompts, nst, groups, dtx_ref, actx_ref, alog_ref, b_ref, enter_ref, skip_ref,
                  gate_ref, out_ref, y_ref):
    rows = length * prompts
    rates = [-jnp.exp(alog_ref[n]) for n in range(nst)]
    skip = skip_ref[...]
    for p in range(prompts):

        def step(t, states):
            row = t * prompts + p
            at = pl.ds(pl.multiple_of(row * groups, groups), groups)
            dt = dtx_ref[at, :]
            act = actx_ref[at, :]
            drive = dt * act
            y = skip * act
            fresh = []
            for n in range(nst):
                s = jnp.exp(dt * rates[n]) * states[n] + drive * b_ref[row * 2 * nst + n]
                y = y + s * b_ref[row * 2 * nst + nst + n]
                fresh.append(s)
            y_ref[at, :] = y
            return tuple(fresh)

        lax.fori_loop(0, length, step, tuple(enter_ref[p, n] for n in range(nst)), unroll=4)
    for k in range(groups):
        cols = pl.ds(k * LANES, LANES)
        gate = gate_ref[:, cols].astype(jnp.float32)
        y = y_ref[pl.ds(k, rows, stride=groups), :]
        out_ref[:, cols] = (y * (gate * jax.nn.sigmoid(gate))).astype(jnp.bfloat16)


def in_vmem(count):
    return [pl.BlockSpec(memory_space=pltpu.VMEM)] * count


def local_states(low, dt_proj, dt_bias, act, alog, bc, prompts):
    rows, channels = act.shape
    groups = channels // LANES
    nst = alog.shape[0]
    body = lambda *refs: state_kernel(rows // prompts, prompts, nst, groups, *refs)
    f32 = jnp.float32
    return pl.pallas_call(
        body,
        out_shape=[
            jax.ShapeDtypeStruct((rows * groups, LANES), f32),
            jax.ShapeDtypeStruct((rows * groups, LANES), f32),
            jax.ShapeDtypeStruct((prompts, nst, groups, LANES), f32),
            jax.ShapeDtypeStruct((prompts, groups, LANES), f32),
        ],
        in_specs=in_vmem(5) + [pl.BlockSpec(memory_space=pltpu.SMEM)],
        out_specs=in_vmem(4),
        compiler_params=pltpu.CompilerParams(vmem_limit_bytes=VMEM_LIMIT),
        name="local_states",
    )(low, dt_proj, dt_bias, act, alog, bc)


def gated_output(dtx, actx, alog, bc, entering, skip, gate):
    rows, channels = gate.shape
    groups = channels // LANES
    prompts, nst = entering.shape[:2]
    body = lambda *refs: output_kernel(rows // prompts, prompts, nst, groups, *refs)
    return pl.pallas_call(
        body,
        out_shape=jax.ShapeDtypeStruct((rows, channels), jnp.bfloat16),
        in_specs=in_vmem(3) + [pl.BlockSpec(memory_space=pltpu.SMEM)] + in_vmem(3),
        out_specs=pl.BlockSpec(memory_space=pltpu.VMEM),
        scratch_shapes=[pltpu.VMEM((rows * groups, LANES), jnp.float32)],
        compiler_params=pltpu.CompilerParams(vmem_limit_bytes=VMEM_LIMIT),
        name="gated_output",
    )(dtx, actx, alog, bc, entering, skip, gate)


def entering_state(totals, states, alog, carry):
    place = lax.axis_index("seq")
    rate = -jnp.exp(alog)
    state = carry
    for j in range(totals.shape[0]):
        later = jnp.exp(rate[None] * totals[j][:, None]) * state + states[j]
        state = jnp.where(j < place, later, state)
    return state


def shards(
    layer_input,
    x_branch,
    gate_branch,
    conv_weight,
    conv_bias,
    x_proj,
    dt_proj,
    dt_bias,
    a_log,
    d_skip,
    carry_state,
    carry_tail,
    out_proj,
    steering,
    refusal,
    norm_gain,
    router,
    specialist_switch_matrix,
    w_up,
    w_down,
    expert_ids,
):
    width = conv_weight.shape[0] - 1
    length, prompts, channels = x_branch.shape
    groups = channels // LANES
    received = passed_along(x_branch[length - width :], "seq", 1)
    leading_shard = lax.axis_index("seq") == 0
    tail = jnp.where(leading_shard, carry_tail, received)
    padded = jnp.concatenate([tail, x_branch], axis=0).astype(jnp.float32)
    convolved = conv_bias.astype(jnp.float32)
    for k in range(conv_weight.shape[0]):
        convolved = convolved + conv_weight[k].astype(jnp.float32) * padded[k : k + length]
    row_count = length * prompts
    activated = jax.nn.silu(convolved).reshape(row_count, channels)
    flat_act = activated.astype(jnp.bfloat16)
    projected = lax.psum(jnp.dot(flat_act, x_proj, preferred_element_type=jnp.float32), "expert")
    low_rank = dt_proj.shape[0]
    state_size = a_log.shape[1]
    low = projected[:, :low_rank].astype(jnp.bfloat16)
    bc = projected[:, low_rank:].reshape(-1)
    alog = a_log.T.reshape(state_size, groups, LANES)
    dtx, actx, state, total = local_states(
        low, dt_proj, dt_bias.reshape(1, channels), activated, alog, bc, prompts
    )
    sent = jnp.concatenate([total[:, None], state], axis=1)
    gathered = lax.all_gather(sent, "seq")
    carry = carry_state.transpose(0, 2, 1).reshape(prompts, state_size, groups, LANES)
    entering = entering_state(gathered[:, :, 0], gathered[:, :, 1:], alog, carry)
    gated = gated_output(
        dtx, actx, alog, bc, entering, d_skip.reshape(groups, LANES), gate_branch.reshape(row_count, channels)
    )
    d_model = out_proj.shape[1]
    mixed = jnp.dot(gated, out_proj, preferred_element_type=jnp.float32)
    steering_clean = remove_directions(steering, refusal)
    owner = lax.axis_index("expert")
    own_length = layer_input.shape[0]
    top_count = expert_ids.shape[-1]
    experts = router.shape[1]
    capacity = row_count * top_count * 5 // (4 * experts)
    row_ids = expert_ids.reshape(row_count, top_count)
    slots = slot_matrix(row_ids, owner, capacity)
    slots16 = slots.astype(jnp.bfloat16)
    own_mixed = lax.psum_scatter(
        mixed.astype(jnp.bfloat16), "expert", scatter_dimension=0, tiled=True
    ).astype(jnp.float32)
    own_residual = (
        layer_input.astype(jnp.float32).reshape(own_length * prompts, d_model) + own_mixed + steering_clean
    )
    own_normed = root_mean_normed(own_residual, norm_gain)
    normed = lax.all_gather(own_normed, "expert", axis=0, tiled=True)
    weight_rows = owner_weight(normed, router, row_ids, owner)
    expert_in = jnp.dot(slots16, normed, preferred_element_type=jnp.float32).astype(jnp.bfloat16)
    slot_weight = jnp.sum(jnp.where(slots, weight_rows[None, :], 0.0), axis=1)
    pieces = lax.all_gather(expert_in, "seq", axis=0, tiled=True)
    gate = jnp.dot(pieces, specialist_switch_matrix[0], preferred_element_type=jnp.float32)
    upward = jnp.dot(pieces, w_up[0], preferred_element_type=jnp.float32)
    hidden = (jax.nn.silu(gate) * upward).astype(jnp.bfloat16)
    expert_out = lax.psum_scatter(
        jnp.dot(hidden, w_down[0], preferred_element_type=jnp.float32).astype(jnp.bfloat16),
        "seq",
        scatter_dimension=0,
        tiled=True,
    ).astype(jnp.float32)
    weighted = (expert_out * slot_weight[:, None]).astype(jnp.bfloat16)
    spread = jnp.dot(slots16.T, weighted, preferred_element_type=jnp.float32).astype(jnp.bfloat16)
    combined = lax.psum_scatter(spread, "expert", scatter_dimension=0, tiled=True)
    return (own_residual + combined.astype(jnp.float32)).reshape(own_length, prompts, d_model)


def solution(mesh):
    return jax.shard_map(
        shards,
        mesh=mesh,
        in_specs=(
            P(("seq", "expert"), None, None),
            P("seq", None, "expert"),
            P("seq", None, "expert"),
            P(None, "expert"),
            P("expert"),
            P("expert", None),
            P(None, "expert"),
            P("expert"),
            P("expert", None),
            P("expert"),
            P(None, "expert", None),
            P(None, None, "expert"),
            P("expert", None),
            P(),
            P(),
            P(),
            P(),
            P("expert", None, "seq"),
            P("expert", None, "seq"),
            P("expert", "seq", None),
            P("seq", None, None),
        ),
        out_specs=P(("seq", "expert"), None, None),
        check_vma=False,
    )
```

profile of v0, /device:TPU:0, one launch (start us, length us, event | category | flops | bytes accessed | tf_op | source)
XLA Modules:
  0.0 312.0 jit_solution(7165455405782213705)
XLA Ops:
  6.5 0.9 slice.127
  7.4 2.4 collective-permute-start
  9.8 0.9 slice_convert_fusion.7
  10.6 0.7 convert_element_type.133
  11.3 0.7 broadcast_select_fusion
  12.1 1.2 maximum_convert_fusion
  13.3 0.9 divide_multiply_fusion
  14.3 0.4 reshape.161.refs_3_
  14.6 2.2 fusion.24
  16.9 38.0 %all-reduce.2.cloned.1.call-done = f32[128,288]{1,0:T(8,128)} async-done(((f32[128,288]{1,0:T(8,128)}), f32[128,288]{1,0:T(8,128)}) %all-reduce.2.cloned.1.call-update) | async-done | bytes 147472 | tf_op jit(solution)/shard_map/psum | solution.py:204
  54.9 0.8 slice.164
  55.8 0.9 slice.279.refs_0_
  56.7 1.0 copy-done.3
  57.7 3.6 %local_states.1 = (f32[1024,128]{1,0:T(8,128)S(1)}, f32[1024,128]{1,0:T(8,128)S(1)}, f32[2,16,8,128]{3,2,1,0:T(8,128)S(1)}, f32[2,8,128]{2,1,0:T(8,128)S(1)}) custom-call(bf16[128,256]{1,0:T(8,128)(2,1)S(1)} %slice.279.refs_0_, bf16[256,1024]{1,0:T(8,128)(2,1)S(1)} %copy-done.3, f32[1,1024]{1,0:T(1,128)S(1)} %bitcast.136, f32[128,1024]{1,0:T(8,128)S(1)} %reshape.161.refs_3_, ...), custom_call_target="tpu_custom_call" | custom-call | tf_op jit(solution)/shard_map/local_states/pallas_call | solution.py:127
  61.4 0.8 copy-done.1
  62.2 0.7 pad_maximum_fusion
  62.9 0.7 multiply_reduce_fusion.13
  64.4 0.9 copy.49
  65.5 21.0 %all-gather.9.cloned.1.call-done = f32[16,17,8,128]{3,2,1,0:T(8,128)} async-done(((f32[2,17,8,128]{3,2,1,0:T(8,128)}), f32[16,17,8,128]{3,2,1,0:T(8,128)}) %all-gather.9.cloned.1.call-update) | async-done | bytes 1114128 | tf_op jit(solution)/shard_map/all_gather | solution.py:214
  86.5 0.8 slice_bitcast_fusion.15
  87.3 1.5 fusion.28.refs_4_
  88.9 1.0 copy-done.2
  89.9 4.0 %gated_output.1 = bf16[128,1024]{1,0:T(8,128)(2,1)S(1)} custom-call(f32[1024,128]{1,0:T(8,128)S(1)} %get-tuple-element.9.refs_0_, f32[1024,128]{1,0:T(8,128)S(1)} %copy-done.2, f32[16,8,128]{2,1,0:T(8,128)S(1)} %bitcast.134, f32[4096]{0:T(1024)S(1)} %reshape.164.refs_5_.refs_3_, f32[2,16,8,128]{3,2,1,0:T(8,128)S(1)} %fusion.28.refs_4_, ...), custom_call_target="tpu_custom_call" | custom-call | tf_op jit(solution)/shard_map/gated_output/pallas_call | solution.py:147
  93.9 5.7 %convolution_convert_fusion.2 = bf16[128,4096]{1,0:T(8,128)(2,1)} fusion(bf16[128,1024]{1,0:T(8,128)(2,1)S(1)} %gated_output.1, bf16[1024,4096]{1,0:T(8,128)(2,1)} %param.33), kind=kOutput, calls=%fused_computation.2 | convolution fusion | flops 1074266112 | bytes 9699328 | tf_op jit(solution)/shard_map/dot_general | solution.py:221
  99.7 0.7 fusion.48
  100.4 1.3 multiply_reduce_fusion.11
  102.4 2.6 multiply_reduce_fusion.10
  105.0 1.8 multiply_reduce_fusion.7
  107.5 3.2 %multiply_reduce_fusion.6 = (f32[]{:T(128)}, f32[]{:T(128)}, f32[4096]{0:T(1024)S(1)}, f32[4096]{0:T(1024)S(1)}) fusion(f32[4096]{0:T(1024)S(1)} %get-tuple-element.29, f32[]{:T(128)S(6)} %rsqrt.22, f32[4096]{0:T(1024)S(1)} %get-tuple-element.31, f32[]{:T(128)S(6)} %rsqrt.21, f32[]{:T(128)} %get-tuple-element.13, f32[4096]{0:T(1024)S(1)} %bitcast.144, ...), kind=kLoop, calls=%fused_computation.86 | loop fusion | flops 61438 | bytes 106528 | tf_op jit(solution)/shard_map/reduce_sum | solution.py:29
  110.7 1.2 multiply_reduce_fusion.2
  112.7 1.2 multiply_reduce_fusion.1
  113.8 1.2 multiply_subtract_fusion
  115.0 11.9 %reduce-scatter.4.cloned.1.call-done = bf16[32,4096]{1,0:T(8,128)(2,1)} async-done(((bf16[128,4096]{1,0:T(8,128)(2,1)}), bf16[32,4096]{1,0:T(8,128)(2,1)}) %reduce-scatter.4.cloned.1.call-update) | async-done | bytes 262160 | tf_op jit(solution)/shard_map/reduce_scatter | solution.py:231
  126.9 1.1 multiply_reduce_fusion
  128.1 1.8 multiply_convert_fusion.2
  130.7 25.9 %all-gather.5.cloned.1.call-done = bf16[128,4096]{1,0:T(8,128)(2,1)} async-done(((bf16[32,4096]{1,0:T(8,128)(2,1)}), bf16[128,4096]{1,0:T(8,128)(2,1)}) %all-gather.5.cloned.1.call-update) | async-done | bytes 1048592 | tf_op jit(solution)/shard_map/all_gather | solution.py:238
  156.6 2.4 convolution_convert_fusion.3
  159.1 0.2 reduce-scatter.6.cloned.1.call-start
  159.3 40.5 %all-gather.7.cloned.1.call-done = bf16[640,4096]{1,0:T(8,128)(2,1)} async-done(((bf16[80,4096]{1,0:T(8,128)(2,1)}), bf16[640,4096]{1,0:T(8,128)(2,1)}) %all-gather.7.cloned.1.call-update) | async-done | bytes 5242896 | tf_op jit(solution)/shard_map/all_gather | solution.py:242
  199.8 5.5 %fusion.3 = f32[640,256]{1,0:T(8,128)} fusion(bf16[640,4096]{1,0:T(8,128)(2,1)} %all-gather.7.cloned.1.call-done, bf16[1,4096,256]{2,1,0:T(8,128)(2,1)} %param.38), kind=kOutput, calls=%fused_computation.7 | convolution fusion | flops 1342177280 | bytes 7995392 | tf_op jit(solution)/shard_map/dot_general | solution.py:243
  205.3 11.1 %convolution_convert_fusion = bf16[640,4096]{1,0:T(8,128)(2,1)} fusion(bf16[1,256,4096]{2,1,0:T(8,128)(2,1)S(1)} %copy-done, bf16[640,4096]{1,0:T(8,128)(2,1)} %all-gather.7.cloned.1.call-done, bf16[1,4096,256]{2,1,0:T(8,128)(2,1)} %param.39, f32[640,256]{1,0:T(8,128)} %fusion.3), kind=kOutput, calls=%fused_computation | convolution fusion | flops 2687959040 | bytes 15335424 | tf_op jit(solution)/shard_map/dot_general | solution.py:247
  216.7 0.4 copy-done.12
  217.1 1.6 fusion.50
  219.0 54.1 %reduce-scatter.6.cloned.1.call-done = bf16[80,4096]{1,0:T(8,128)(2,1)} async-done(((bf16[640,4096]{1,0:T(8,128)(2,1)}), bf16[80,4096]{1,0:T(8,128)(2,1)}) %reduce-scatter.6.cloned.1.call-update) | async-done | bytes 655376 | tf_op jit(solution)/shard_map/reduce_scatter | solution.py:246
  273.2 2.6 convolution_convert_fusion.1
  275.8 27.3 %reduce-scatter.8.cloned.1.call-done = bf16[32,4096]{1,0:T(8,128)(2,1)} async-done(((bf16[128,4096]{1,0:T(8,128)(2,1)}), bf16[32,4096]{1,0:T(8,128)(2,1)}) %reduce-scatter.8.cloned.1.call-update) | async-done | bytes 262160 | tf_op jit(solution)/shard_map/reduce_scatter | solution.py:254
  303.1 1.0 convert_add_fusion
  304.1 1.1 reshape.168
  (66 shorter events, 2.0 us)
Async XLA Ops:
  6.5 198.8 %copy-start = (bf16[1,256,4096]{2,1,0:T(8,128)(2,1)S(1)}, bf16[1,256,4096]{2,1,0:T(8,128)(2,1)}, u32[]{:S(2)}) copy-start(bf16[1,256,4096]{2,1,0:T(8,128)(2,1)} %param.40) | copy-start | bytes 6291460
  6.5 48.3 %all-reduce.2.cloned.1.call-start = ((), (), s32[]{:S(2)}) async-start(), calls=%async_computation.3 | async-start | bytes 393216 | tf_op jit(solution)/shard_map/psum | solution.py:204
  7.4 3.9 %collective-permute-start = (bf16[3,2,1024]{2,1,0:T(2,128)(2,1)S(1)}, bf16[3,2,1024]{2,1,0:T(2,128)(2,1)S(1)}, u32[]{:S(2)}, u32[]{:S(2)}) collective-permute-start(bf16[3,2,1024]{2,1,0:T(2,128)(2,1)S(1)} %slice.127), channel_id=1, source_target_pairs={{0,4},{4,8},{8,12},{12,16},{16,20},{20,24},{24,28},{1,5},{5,9},{9,... | collective-permute-start | bytes 36872 | tf_op jit(solution)/shard_map/ppermute | solution.py:16
  13.3 3.6 %copy-start.11 = (f32[1024,16]{0,1:T(8,128)S(1)}, f32[1024,16]{0,1:T(8,128)}, u32[]{:S(2)}) copy-start(f32[1024,16]{0,1:T(8,128)} %param.29) | copy-start | bytes 196612
  14.2 42.5 %copy-start.4 = (f32[1024]{0:T(1024)S(1)}, f32[1024]{0:T(1024)}, u32[]{:S(2)}) copy-start(f32[1024]{0:T(1024)} %param.28) | copy-start | bytes 12292
  14.2 48.7 %copy-start.9 = (bf16[4,4096]{1,0:T(4,128)(2,1)S(1)}, bf16[4,4096]{1,0:T(4,128)(2,1)}, u32[]{:S(2)}) copy-start(bf16[4,4096]{1,0:T(4,128)(2,1)} %param.35) | copy-start | bytes 98308
  14.2 50.1 %copy-start.13 = (bf16[4096]{0:T(1024)(128)(2,1)S(1)}, bf16[4096]{0:T(1024)(128)(2,1)}, u32[]{:S(2)}) copy-start(bf16[4096]{0:T(1024)(128)(2,1)} %param.36) | copy-start | bytes 24580
  14.6 50.7 %copy-start.8 = (bf16[64,2,1024]{2,1,0:T(2,128)(2,1)S(1)}, bf16[64,2,1024]{2,1,0:T(2,128)(2,1)}, u32[]{:S(2)}) copy-start(bf16[64,2,1024]{2,1,0:T(2,128)(2,1)} %param.23) | copy-start | bytes 786436
  16.8 69.7 %all-gather.9.cloned.1.call-start = ((), (), s32[]{:S(2)}) async-start(), calls=%async_computation.9 | async-start | bytes 1253376 | tf_op jit(solution)/shard_map/all_gather | solution.py:214
  56.7 1.0 copy-start.3
  57.7 31.1 %copy-start.5 = (f32[1024]{0:T(1024)S(1)}, f32[1024]{0:T(1024)}, u32[]{:S(2)}) copy-start(f32[1024]{0:T(1024)} %param.30) | copy-start | bytes 12292
  61.4 0.8 copy-start.1
  62.9 64.1 %reduce-scatter.4.cloned.1.call-start = ((), (), s32[]{:S(2)}) async-start(), calls=%async_computation.4 | async-start | bytes 1310720 | tf_op jit(solution)/shard_map/reduce_scatter | solution.py:231
  88.9 1.0 copy-start.2
  93.9 5.8 %copy-start.10 = (bf16[4096]{0:T(1024)(128)(2,1)S(1)}, bf16[4096]{0:T(1024)(128)(2,1)}, u32[]{:S(2)}) copy-start(bf16[4096]{0:T(1024)(128)(2,1)} %param.34) | copy-start | bytes 24580
  93.9 18.6 %copy-start.7 = (bf16[16,2,4096]{2,1,0:T(2,128)(2,1)S(1)}, bf16[16,2,4096]{2,1,0:T(2,128)(2,1)}, u32[]{:S(2)}) copy-start(bf16[16,2,4096]{2,1,0:T(2,128)(2,1)} %param.21) | copy-start | bytes 786436
  99.6 30.3 %copy-start.14 = (s32[64,2,2]{0,2,1:T(2,128)S(1)}, s32[64,2,2]{0,2,1:T(2,128)}, u32[]{:S(2)}) copy-start(s32[64,2,2]{0,2,1:T(2,128)} %param.41) | copy-start | bytes 3076
  99.7 57.0 %all-gather.5.cloned.1.call-start = ((), (), s32[]{:S(2)}) async-start(), calls=%async_computation.5 | async-start | bytes 1310720 | tf_op jit(solution)/shard_map/all_gather | solution.py:238
  129.9 69.9 %all-gather.7.cloned.1.call-start = ((), (), s32[]{:S(2)}) async-start(), calls=%async_computation.6 | async-start | bytes 5898240 | tf_op jit(solution)/shard_map/all_gather | solution.py:242
  159.1 114.1 %reduce-scatter.6.cloned.1.call-start = ((), (), s32[]{:S(2)}) async-start(), calls=%async_computation.7 | async-start | bytes 5898240 | tf_op jit(solution)/shard_map/reduce_scatter | solution.py:246
  216.4 0.8 copy-start.12
  216.4 86.6 %copy-start.6 = (bf16[32,4096]{1,0:T(8,128)(2,1)S(1)}, bf16[32,4096]{1,0:T(8,128)(2,1)}, u32[]{:S(2)}) copy-start(bf16[32,4096]{1,0:T(8,128)(2,1)} %reduce-scatter.4.cloned.1.call-done) | copy-start | bytes 786436
  216.4 86.6 %reduce-scatter.8.cloned.1.call-start = ((), (), s32[]{:S(2)}) async-start(), calls=%async_computation.8 | async-start | bytes 1310720 | tf_op jit(solution)/shard_map/reduce_scatter | solution.py:254
Sparse Core Ops, SparseCore 0:
  16.9 37.8 all-reduce.1
  63.0 23.4 all-gather.8
  99.8 27.1 reduce-scatter.3
  130.0 26.5 all-gather.4
  159.2 40.6 all-gather.6
  216.5 56.5 reduce-scatter.5
  275.9 27.1 reduce-scatter.7
where the time goes:
time: 313 us; the launch traced here: 312 us
  waiting for transfers between devices  219 us (70%)
  matrix products  31 us (10%)
  other arithmetic  25.1 us (8%)
  between operations  16.7 us (5%)
  local copies, waits for them, and re-layouts  10.1 us (3%)
  Pallas kernels  7.62 us (2%)
    reduce_scatter x1, waiting for transfers between devices, shards(): lax.psum_scatter(jnp.dot(hidden, w_down[0], preferred_element_type=jnp.fl...  54.1 us
    all_gather x1, waiting for transfers between devices, shards(): pieces = lax.all_gather(expert_in, 'seq', axis=0, tiled=True)  40.5 us
    psum x1, waiting for transfers between devices, shards(): lax.psum(jnp.dot(flat_act, x_proj, preferred_element_type=jnp.float32), '...  38 us
    reduce_scatter x1, waiting for transfers between devices, shards(): lax.psum_scatter(spread, 'expert', scatter_dimension=0, tiled=True)  27.3 us
    all_gather x1, waiting for transfers between devices, shards(): normed = lax.all_gather(own_normed, 'expert', axis=0, tiled=True)  25.9 us
    all_gather x1, waiting for transfers between devices, shards(): gathered = lax.all_gather(sent, 'seq')  21 us
    reduce_scatter x1, waiting for transfers between devices, shards(): lax.psum_scatter(mixed.astype(jnp.bfloat16), 'expert', scatter_dimension=...  11.9 us
    dot_general x1, matrix products, shards(): jnp.dot(hidden, w_down[0], preferred_element_type=jnp.float32)  11.1 us
  transfers between devices with their start and end apart: 8, of which 7 were waited for; matrix products, arithmetic and copies ran while one was open for 6% of the time, Pallas kernels for 0%

commit v1 on v0

--- a/solution.py
+++ b/solution.py
@@ -153,6 +153,228 @@
         compiler_params=pltpu.CompilerParams(vmem_limit_bytes=VMEM_LIMIT),
         name="gated_output",
     )(dtx, actx, alog, bc, entering, skip, gate)
+
+
+def greet(devices):
+    barrier = pltpu.get_barrier_semaphore()
+    for device in devices:
+        pl.semaphore_signal(barrier, inc=1, device_id=device, device_id_type=pl.DeviceIdType.MESH)
+    pl.semaphore_wait(barrier, len(devices))
+
+
+def push(source, target, sends, receives, slot, device):
+    return pltpu.make_async_remote_copy(
+        src_ref=source,
+        dst_ref=target,
+        send_sem=sends.at[slot],
+        recv_sem=receives.at[slot],
+        device_id=device,
+        device_id_type=pl.DeviceIdType.MESH,
+    )
+
+
+def chip_places(seq_count):
+    chips = seq_count // 2
+    place = lax.axis_index("seq")
+    expert = lax.axis_index("expert")
+    chip = place // 2
+    core = place % 2
+    sibling = (chip * 2 + 1 - core, expert)
+
+    def ahead(step):
+        return ((chip + step) % chips * 2 + core, expert)
+
+    return chips, chip, core, sibling, ahead
+
+
+def expert_sum_kernel(count, part_ref, out_ref, got, send_a, recv_a, send_b, recv_b):
+    place = lax.axis_index("seq")
+    me = lax.axis_index("expert")
+    block = part_ref.shape[0] // count
+    peers = [((place, (me + r) % count), (me + r) % count) for r in range(1, count)]
+    greet([device for device, _ in peers])
+    mine = pl.ds(pl.multiple_of(me * block, block), block)
+    first = []
+    for r, (device, other) in enumerate(peers):
+        rows = pl.ds(pl.multiple_of(other * block, block), block)
+        copy = push(part_ref.at[rows], got.at[r], send_a, recv_a, r, device)
+        copy.start()
+        first.append(copy)
+    total = part_ref[mine, :]
+    for r, copy in enumerate(first):
+        copy.wait_recv()
+        total = total + got[r]
+    out_ref[mine, :] = total
+    second = []
+    for r, (device, _) in enumerate(peers):
+        copy = push(out_ref.at[mine], out_ref.at[mine], send_b, recv_b, r, device)
+        copy.start()
+        second.append(copy)
+    for copy in second:
+        copy.wait_recv()
+    for copy in first + second:
+        copy.wait_send()
+
+
+def expert_sum(part):
+    count = lax.axis_size("expert")
+    rows, width = part.shape
+    dma = pltpu.SemaphoreType.DMA((count - 1,))
+    return pl.pallas_call(
+        lambda *refs: expert_sum_kernel(count, *refs),
+        out_shape=jax.ShapeDtypeStruct(part.shape, part.dtype),
+        in_specs=in_vmem(1),
+        out_specs=pl.BlockSpec(memory_space=pltpu.VMEM),
+        scratch_shapes=[pltpu.VMEM((count - 1, rows // count, width), part.dtype)] + [dma] * 4,
+        compiler_params=pltpu.CompilerParams(
+            collective_id=0, has_side_effects=True, vmem_limit_bytes=VMEM_LIMIT
+        ),
+        name="expert_sum",
+    )(part)
+
+
+def state_gather_kernel(seq_count, part_ref, out_ref, send_x, recv_x, send_f, recv_f):
+    chips, chip, core, sibling, ahead = chip_places(seq_count)
+    greet([sibling] + [ahead(r) for r in range(1, chips)])
+    me = chip * 2 + core
+    copies = []
+    for r in range(1, chips):
+        copy = push(part_ref, out_ref.at[me], send_x, recv_x, r, ahead(r))
+        copy.start()
+        copies.append(copy)
+    forward = push(part_ref, out_ref.at[me], send_f, recv_f, 0, sibling)
+    forward.start()
+    forwards = [forward]
+    out_ref[me] = part_ref[...]
+    for r in range(1, chips):
+        copies[r - 1].wait_recv()
+        source = (chip - r + chips) % chips * 2 + core
+        forward = push(out_ref.at[source], out_ref.at[source], send_f, recv_f, r, sibling)
+        forward.start()
+        forwards.append(forward)
+    for forward in forwards:
+        forward.wait_recv()
+    for copy in copies + forwards:
+        copy.wait_send()
+
+
+def state_gather(part):
+    seq_count = lax.axis_size("seq")
+    dma = pltpu.SemaphoreType.DMA((seq_count // 2,))
+    return pl.pallas_call(
+        lambda *refs: state_gather_kernel(seq_count, *refs),
+        out_shape=jax.ShapeDtypeStruct((seq_count,) + part.shape, part.dtype),
+        in_specs=in_vmem(1),
+        out_specs=pl.BlockSpec(memory_space=pltpu.VMEM),
+        scratch_shapes=[dma] * 4,
+        compiler_params=pltpu.CompilerParams(
+            collective_id=1, has_side_effects=True, vmem_limit_bytes=VMEM_LIMIT
+        ),
+        name="state_gather",
+    )(part)
+
+
+def experts_kernel(seq_count, x_ref, gate_ref, up_ref, down_ref, out_ref, pieces, mine, theirs, beside,
+                   arrived, send_x, recv_x, send_f, recv_f, send_p, recv_p, send_o, recv_o):
+    chips, chip, core, sibling, ahead = chip_places(seq_count)
+    cap, d_model = x_ref.shape
+    chunk = 512
+    greet([sibling] + [ahead(r) for r in range(1, chips)])
+
+    def tokens(r):
+        return push(x_ref, pieces.at[r, 0], send_x, recv_x, r, ahead(r))
+
+    def handed(r):
+        return push(pieces.at[r, 0], pieces.at[r, 1], send_f, recv_f, r, sibling)
+
+    def within(r):
+        return push(theirs.at[r], beside.at[r], send_p, recv_p, r, sibling)
+
+    def back(r):
+        return push(mine.at[r], arrived.at[r], send_o, recv_o, r, ahead(chips - r))
+
+    for r in range(1, chips):
+        tokens(r).start()
+    pieces[0, 0] = x_ref[...]
+    handed(0).start()
+
+    def compute(r):
+        rows = pieces[r].reshape(2 * cap, d_model)
+        gate = jnp.dot(rows, gate_ref[...], preferred_element_type=jnp.float32)
+        upward = jnp.dot(rows, up_ref[...], preferred_element_type=jnp.float32)
+        hidden = (gate * jax.nn.sigmoid(gate) * upward).astype(jnp.bfloat16)
+
+        def columns(j, _):
+            cols = pl.ds(pl.multiple_of(j * chunk, chunk), chunk)
+            part = jnp.dot(hidden, down_ref[:, cols], preferred_element_type=jnp.float32).astype(
+                jnp.bfloat16
+            )
+            mine[r, :, cols] = part[:cap]
+            theirs[r, :, cols] = part[cap:]
+            return 0
+
+        lax.fori_loop(0, d_model // chunk, columns, 0)
+        within(r).start()
+
+    handed(0).wait_recv()
+    compute(0)
+
+    def turn(r, _):
+        tokens(r).wait_recv()
+        handed(r).start()
+        handed(r).wait_recv()
+        compute(r)
+        within(r).wait_recv()
+
+        def add(j, _):
+            cols = pl.ds(pl.multiple_of(j * chunk, chunk), chunk)
+            total = mine[r, :, cols].astype(jnp.float32) + beside[r, :, cols].astype(jnp.float32)
+            mine[r, :, cols] = total.astype(jnp.bfloat16)
+            return 0
+
+        lax.fori_loop(0, d_model // chunk, add, 0)
+        back(r).start()
+        return 0
+
+    lax.fori_loop(1, chips, turn, 0)
+    within(0).wait_recv()
+    for r in range(1, chips):
+        back(r).wait_recv()
+
+    def finish(j, _):
+        cols = pl.ds(pl.multiple_of(j * chunk, chunk), chunk)
+        total = mine[0, :, cols].astype(jnp.float32) + beside[0, :, cols].astype(jnp.float32)
+        for r in range(1, chips):
+            total = total + arrived[r, :, cols].astype(jnp.float32)
+        out_ref[:, cols] = total
+        return 0
+
+    lax.fori_loop(0, d_model // chunk, finish, 0)
+    for r in range(chips):
+        handed(r).wait_send()
+        within(r).wait_send()
+        if r > 0:
+            tokens(r).wait_send()
+            back(r).wait_send()
+
+
+def run_experts(x, gate, up, down):
+    seq_count = lax.axis_size("seq")
+    chips = seq_count // 2
+    cap, d_model = x.shape
+    dma = pltpu.SemaphoreType.DMA((chips,))
+    block = pltpu.VMEM((chips, cap, d_model), jnp.bfloat16)
+    return pl.pallas_call(
+        lambda *refs: experts_kernel(seq_count, *refs),
+        out_shape=jax.ShapeDtypeStruct((cap, d_model), jnp.float32),
+        in_specs=in_vmem(4),
+        out_specs=pl.BlockSpec(memory_space=pltpu.VMEM),
+        scratch_shapes=[pltpu.VMEM((chips, 2, cap, d_model), jnp.bfloat16)] + [block] * 4 + [dma] * 8,
+        compiler_params=pltpu.CompilerParams(
+            collective_id=2, has_side_effects=True, vmem_limit_bytes=60 * 1024 * 1024
+        ),
+        name="experts",
+    )(x, gate, up, down)
 
 
 def entering_state(totals, states, alog, carry):
@@ -201,7 +423,7 @@
     row_count = length * prompts
     activated = jax.nn.silu(convolved).reshape(row_count, channels)
     flat_act = activated.astype(jnp.bfloat16)
-    projected = lax.psum(jnp.dot(flat_act, x_proj, preferred_element_type=jnp.float32), "expert")
+    projected = expert_sum(jnp.dot(flat_act, x_proj, preferred_element_type=jnp.float32))
     low_rank = dt_proj.shape[0]
     state_size = a_log.shape[1]
     low = projected[:, :low_rank].astype(jnp.bfloat16)
@@ -211,7 +433,7 @@
         low, dt_proj, dt_bias.reshape(1, channels), activated, alog, bc, prompts
     )
     sent = jnp.concatenate([total[:, None], state], axis=1)
-    gathered = lax.all_gather(sent, "seq")
+    gathered = state_gather(sent)
     carry = carry_state.transpose(0, 2, 1).reshape(prompts, state_size, groups, LANES)
     entering = entering_state(gathered[:, :, 0], gathered[:, :, 1:], alog, carry)
     gated = gated_output(
@@ -225,6 +447,7 @@
     top_count = expert_ids.shape[-1]
     experts = router.shape[1]
     capacity = row_count * top_count * 5 // (4 * experts)
+    capacity = (capacity + 15) // 16 * 16
     row_ids = expert_ids.reshape(row_count, top_count)
     slots = slot_matrix(row_ids, owner, capacity)
     slots16 = slots.astype(jnp.bfloat16)
@@ -239,16 +462,7 @@
     weight_rows = owner_weight(normed, router, row_ids, owner)
     expert_in = jnp.dot(slots16, normed, preferred_element_type=jnp.float32).astype(jnp.bfloat16)
     slot_weight = jnp.sum(jnp.where(slots, weight_rows[None, :], 0.0), axis=1)
-    pieces = lax.all_gather(expert_in, "seq", axis=0, tiled=True)
-    gate = jnp.dot(pieces, specialist_switch_matrix[0], preferred_element_type=jnp.float32)
-    upward = jnp.dot(pieces, w_up[0], preferred_element_type=jnp.float32)
-    hidden = (jax.nn.silu(gate) * upward).astype(jnp.bfloat16)
-    expert_out = lax.psum_scatter(
-        jnp.dot(hidden, w_down[0], preferred_element_type=jnp.float32).astype(jnp.bfloat16),
-        "seq",
-        scatter_dimension=0,
-        tiled=True,
-    ).astype(jnp.float32)
+    expert_out = run_experts(expert_in, specialist_switch_matrix[0], w_up[0], w_down[0])
     weighted = (expert_out * slot_weight[:, None]).astype(jnp.bfloat16)
     spread = jnp.dot(slots16.T, weighted, preferred_element_type=jnp.float32).astype(jnp.bfloat16)
     combined = lax.psum_scatter(spread, "expert", scatter_dimension=0, tiled=True)

time: 313 us -> 232 us (0.74)
  waiting for transfers between devices: 219 us -> 62.8 us
  Pallas kernels: 7.62 us -> 106 us
  matrix products: 31 us -> 12.9 us
  local copies, waits for them, and re-layouts: 10.1 us -> 5.99 us
    pallas_call x0 -> x3, Pallas kernels: none -> 98.6 us  [the longest x1 72.9 us: run_experts(): pl.pallas_call(lambda *refs: experts_kernel(seq_count, *refs), out_shape=...]
    all_gather x2 -> x0, waiting for transfers between devices: 61.5 us -> none  [the longest x1 40.5 us: shards(): pieces = lax.all_gather(expert_in, 'seq', axis=0, tiled=True)]
    reduce_scatter x1 -> x0, waiting for transfers between devices: 54.1 us -> none  [shards(): lax.psum_scatter(jnp.dot(hidden, w_down[0], preferred_element_type=jnp.fl...]
    psum x1 -> x0, waiting for transfers between devices: 38 us -> none  [shards(): lax.psum(jnp.dot(flat_act, x_proj, preferred_element_type=jnp.float32), '...]
    dot_general x2 -> x0, matrix products: 16.6 us -> none  [the longest x1 11.1 us: shards(): jnp.dot(hidden, w_down[0], preferred_element_type=jnp.float32)]
  transfers between devices with their start and end apart: 8 -> 4, of which waited for: 7 -> 3; matrix products, arithmetic and copies ran while one was open for 6% -> 9% of each run, Pallas kernels for 0% -> 0%
where the time goes in v1:
time: 232 us; the launch traced here: 231 us
  Pallas kernels  106 us (46%)
  waiting for transfers between devices  62.8 us (27%)
  other arithmetic  24.7 us (11%)
  between operations  16.3 us (7%)
  matrix products  12.9 us (6%)
  local copies, waits for them, and re-layouts  5.99 us (3%)
  starting transfers between devices  2.44 us (1%)
    pallas_call x1, Pallas kernels, run_experts(): pl.pallas_call(lambda *refs: experts_kernel(seq_count, *refs), out_shape=...  72.9 us
    all_gather x1, waiting for transfers between devices, shards(): normed = lax.all_gather(own_normed, 'expert', axis=0, tiled=True)  25.7 us
    reduce_scatter x1, waiting for transfers between devices, shards(): lax.psum_scatter(spread, 'expert', scatter_dimension=0, tiled=True)  25.3 us
    pallas_call x1, Pallas kernels, expert_sum(): pl.pallas_call(lambda *refs: expert_sum_kernel(count, *refs), out_shape=j...  15.7 us
    reduce_scatter x1, waiting for transfers between devices, shards(): lax.psum_scatter(mixed.astype(jnp.bfloat16), 'expert', scatter_dimension=...  11.8 us
    pallas_call x1, Pallas kernels, state_gather(): pl.pallas_call(lambda *refs: state_gather_kernel(seq_count, *refs), out_s...  10 us
    reduce_sum x4, other arithmetic, remove_directions(): vector = vector - jnp.sum(q * vector) * q  7.63 us
    dot_general x1, matrix products, shards(): mixed = jnp.dot(gated, out_proj, preferred_element_type=jnp.float32)  5.69 us
  transfers between devices with their start and end apart: 4, of which 3 were waited for; matrix products, arithmetic and copies ran while one was open for 9% of the time, Pallas kernels for 0%

profile of v1, /device:TPU:0, one launch (start us, length us, event | category | flops | bytes accessed | tf_op | source)
XLA Modules:
  0.0 231.3 jit_solution(16711138131484244635)
XLA Ops:
  6.5 0.8 slice.127
  7.3 2.4 %collective-permute-start = (bf16[3,2,1024]{2,1,0:T(2,128)(2,1)S(1)}, bf16[3,2,1024]{2,1,0:T(2,128)(2,1)S(1)}, u32[]{:S(2)}, u32[]{:S(2)}) collective-permute-start(bf16[3,2,1024]{2,1,0:T(2,128)(2,1)S(1)} %slice.127), channel_id=1, source_target_pairs={{0,4},{4,8},{8,12},{12,16},{16,20},{20,24},{24,28},{1,5},{5,9},{9,... | collective-permute-start | bytes 36872 | tf_op jit(solution)/shard_map/ppermute | solution.py:16
  9.7 0.9 slice_convert_fusion.7
  10.6 0.9 copy.44
  11.4 0.9 slice_convert_fusion.2
  12.4 1.4 multiply_reduce_fusion.13
  13.8 0.7 convert_element_type.124
  14.4 0.9 copy.45
  15.4 1.1 reshape.167.refs_6_
  17.1 0.7 broadcast_select_fusion
  17.9 1.2 maximum_convert_fusion
  19.1 0.9 divide_multiply_fusion
  20.0 0.4 reshape.161.refs_3_
  20.4 0.4 fusion.5.refs_0_
  20.8 15.7 %expert_sum.1 = f32[128,288]{1,0:T(8,128)S(1)} custom-call(f32[128,288]{1,0:T(8,128)S(1)} %fusion.5.refs_0_), custom_call_target="tpu_custom_call" | custom-call | tf_op jit(solution)/shard_map/expert_sum/pallas_call | solution.py:223
  36.6 3.6 %local_states.1 = (f32[1024,128]{1,0:T(8,128)S(1)}, f32[1024,128]{1,0:T(8,128)S(1)}, f32[2,16,8,128]{3,2,1,0:T(8,128)S(1)}, f32[2,8,128]{2,1,0:T(8,128)S(1)}) custom-call(bf16[128,256]{1,0:T(8,128)(2,1)S(1)} %slice.218.refs_0_, bf16[256,1024]{1,0:T(8,128)(2,1)S(1)} %copy-done.1, f32[1,1024]{1,0:T(1,128)S(1)} %bitcast.103, f32[128,1024]{1,0:T(8,128)S(1)} %reshape.161.refs_3_, ...), custom_call_target="tpu_custom_call" | custom-call | tf_op jit(solution)/shard_map/local_states/pallas_call | solution.py:127
  40.3 10.0 %state_gather.1 = f32[8,2,17,8,128]{4,3,2,1,0:T(8,128)S(1)} custom-call(f32[2,17,8,128]{3,2,1,0:T(8,128)S(1)} %pad_maximum_fusion.refs_0_), custom_call_target="tpu_custom_call" | custom-call | tf_op jit(solution)/shard_map/state_gather/pallas_call | solution.py:264
  50.3 0.2 fusion.8.refs_4_
  50.5 4.0 %gated_output.1 = bf16[128,1024]{1,0:T(8,128)(2,1)S(1)} custom-call(f32[1024,128]{1,0:T(8,128)S(1)} %get-tuple-element.9.refs_0_, f32[1024,128]{1,0:T(8,128)S(1)} %get-tuple-element.10.refs_1_, f32[16,8,128]{2,1,0:T(8,128)S(1)} %bitcast.101, f32[4096]{0:T(1024)S(1)} %reshape.164.refs_5_.refs_3_, f32[2,16,8,128]{3,2,1,0:T(8,128)S(1)} %fusion.8.refs_4_, ...), custom_call_target="tpu_custom_call" | custom-call | tf_op jit(solution)/shard_map/gated_output/pallas_call | solution.py:147
  54.6 5.7 %convolution_convert_fusion.1 = bf16[128,4096]{1,0:T(8,128)(2,1)} fusion(bf16[128,1024]{1,0:T(8,128)(2,1)S(1)} %gated_output.1, bf16[1024,4096]{1,0:T(8,128)(2,1)} %param.33), kind=kOutput, calls=%fused_computation.1 | convolution fusion | flops 1074266112 | bytes 9699328 | tf_op jit(solution)/shard_map/dot_general | solution.py:443
  60.4 0.7 fusion.22
  61.1 1.3 multiply_reduce_fusion.11
  63.1 2.6 %multiply_reduce_fusion.10 = (f32[]{:T(128)}, f32[]{:T(128)}, f32[]{:T(128)}) fusion(f32[4096]{0:T(1024)S(1)} %get-tuple-element.31, f32[4096]{0:T(1024)S(1)} %bitcast.110, bf16[4096]{0:T(1024)(128)(2,1)S(1)} %copy-done.7, f32[]{:T(128)S(6)} %rsqrt.21, f32[]{:T(128)} %get-tuple-element.18, f32[4096]{0:T(1024)S(1)} %bitcast.118, f32[]{:T(128)} %get-tuple-element.20, ...), kind=kLoop, calls=%fused_computation.72 | loop fusion | flops 57341 | bytes 73756 | tf_op jit(solution)/shard_map/reduce_sum | solution.py:29
  65.7 1.8 multiply_reduce_fusion.7
  68.2 3.2 %multiply_reduce_fusion.6 = (f32[]{:T(128)}, f32[]{:T(128)}, f32[4096]{0:T(1024)S(1)}, f32[4096]{0:T(1024)S(1)}) fusion(f32[4096]{0:T(1024)S(1)} %get-tuple-element.29, f32[]{:T(128)S(6)} %rsqrt.22, f32[4096]{0:T(1024)S(1)} %get-tuple-element.31, f32[]{:T(128)S(6)} %rsqrt.21, f32[]{:T(128)} %get-tuple-element.13, f32[4096]{0:T(1024)S(1)} %bitcast.112, ...), kind=kLoop, calls=%fused_computation.64 | loop fusion | flops 61438 | bytes 106528 | tf_op jit(solution)/shard_map/reduce_sum | solution.py:29
  71.4 1.2 multiply_reduce_fusion.2
  73.4 1.2 multiply_reduce_fusion.1
  74.5 1.2 multiply_subtract_fusion
  75.8 11.8 %reduce-scatter.3.cloned.1.call-done = bf16[32,4096]{1,0:T(8,128)(2,1)} async-done(((bf16[128,4096]{1,0:T(8,128)(2,1)}), bf16[32,4096]{1,0:T(8,128)(2,1)}) %reduce-scatter.3.cloned.1.call-update) | async-done | bytes 262160 | tf_op jit(solution)/shard_map/reduce_scatter | solution.py:454
  87.5 1.1 multiply_reduce_fusion
  88.7 1.8 multiply_convert_fusion.2
  90.5 0.1 copy.42
  90.7 0.1 copy.41
  90.8 0.1 eq.54
  90.9 0.1 copy.39
  91.1 0.2 reduce-window.8
  91.3 0.1 and.12
  91.4 0.1 add_reduce_fusion
  91.5 25.7 %all-gather.2.cloned.1.call-done = bf16[128,4096]{1,0:T(8,128)(2,1)} async-done(((bf16[32,4096]{1,0:T(8,128)(2,1)}), bf16[128,4096]{1,0:T(8,128)(2,1)}) %all-gather.2.cloned.1.call-update) | async-done | bytes 1048592 | tf_op jit(solution)/shard_map/all_gather | solution.py:461
  117.2 1.6 fusion.23
  118.9 0.1 multiply_reduce_fusion.14
  119.0 0.1 select_reduce_fusion
  119.1 2.4 %convolution_convert_fusion.2.refs_0_ = bf16[80,4096]{1,0:T(8,128)(2,1)} fusion(bf16[128,4096]{1,0:T(8,128)(2,1)} %all-gather.2.cloned.1.call-done, s32[128]{0:T(128)S(1)} %add_reduce_fusion, pred[128]{0:T(512)(128)(4,1)S(1)} %and.12), kind=kOutput, calls=%fused_computation.2 | convolution fusion | flops 84234240 | bytes 1704576 | tf_op jit(solution)/shard_map/dot_general | solution.py:463
  121.5 72.9 %experts.1 = f32[80,4096]{1,0:T(8,128)} custom-call(bf16[80,4096]{1,0:T(8,128)(2,1)} %convolution_convert_fusion.2.refs_0_, bf16[4096,256]{1,0:T(8,128)(2,1)} %bitcast.105, bf16[4096,256]{1,0:T(8,128)(2,1)} %bitcast.106, bf16[256,4096]{1,0:T(8,128)(2,1)} %bitcast.107), custom_call_target="tpu_custom_call" | custom-call | tf_op jit(solution)/shard_map/experts/pallas_call | solution.py:367
  194.5 2.9 %convolution_convert_fusion = bf16[128,4096]{1,0:T(8,128)(2,1)} fusion(f32[80,4096]{1,0:T(8,128)} %experts.1, f32[80]{0:T(128)S(1)} %select_reduce_fusion, s32[128]{0:T(128)S(1)} %add_reduce_fusion, pred[128]{0:T(512)(128)(4,1)S(1)} %and.12), kind=kOutput, calls=%fused_computation | convolution fusion | flops 85086208 | bytes 2360256 | tf_op jit(solution)/shard_map/dot_general | solution.py:467
  197.3 25.3 %reduce-scatter.5.cloned.1.call-done = bf16[32,4096]{1,0:T(8,128)(2,1)} async-done(((bf16[128,4096]{1,0:T(8,128)(2,1)}), bf16[32,4096]{1,0:T(8,128)(2,1)}) %reduce-scatter.5.cloned.1.call-update) | async-done | bytes 262160 | tf_op jit(solution)/shard_map/reduce_scatter | solution.py:468
  222.6 1.0 convert_add_fusion
  223.7 1.1 reshape.168
  (47 shorter events, 0.6 us)
Async XLA Ops:
  6.5 13.9 %copy-start = (bf16[1024,288]{0,1:T(8,128)(2,1)S(1)}, bf16[1024,288]{0,1:T(8,128)(2,1)}, u32[]{:S(2)}) copy-start(bf16[1024,288]{0,1:T(8,128)(2,1)} %param.26) | copy-start | bytes 1769476
  6.5 81.0 %reduce-scatter.3.cloned.1.call-start = ((), (), s32[]{:S(2)}) async-start(), calls=%async_computation.2 | async-start | bytes 1310720 | tf_op jit(solution)/shard_map/reduce_scatter | solution.py:454
  7.3 9.8 %collective-permute-start = (bf16[3,2,1024]{2,1,0:T(2,128)(2,1)S(1)}, bf16[3,2,1024]{2,1,0:T(2,128)(2,1)S(1)}, u32[]{:S(2)}, u32[]{:S(2)}) collective-permute-start(bf16[3,2,1024]{2,1,0:T(2,128)(2,1)S(1)} %slice.127), channel_id=1, source_target_pairs={{0,4},{4,8},{8,12},{12,16},{16,20},{20,24},{24,28},{1,5},{5,9},{9,... | collective-permute-start | bytes 36872 | tf_op jit(solution)/shard_map/ppermute | solution.py:16
  20.0 16.6 %copy-start.1 = (bf16[256,1024]{1,0:T(8,128)(2,1)S(1)}, bf16[256,1024]{1,0:T(8,128)(2,1)}, u32[]{:S(2)}) copy-start(bf16[256,1024]{1,0:T(8,128)(2,1)} %refs_1_.1) | copy-start | bytes 1572868
  20.0 16.6 %copy-start.2 = (f32[1024]{0:T(1024)S(1)}, f32[1024]{0:T(1024)}, u32[]{:S(2)}) copy-start(f32[1024]{0:T(1024)} %param.28) | copy-start | bytes 12292
  36.6 13.9 %copy-start.3 = (f32[1024]{0:T(1024)S(1)}, f32[1024]{0:T(1024)}, u32[]{:S(2)}) copy-start(f32[1024]{0:T(1024)} %param.30) | copy-start | bytes 12292
  54.6 5.8 %copy-start.6 = (bf16[4,4096]{1,0:T(4,128)(2,1)S(1)}, bf16[4,4096]{1,0:T(4,128)(2,1)}, u32[]{:S(2)}) copy-start(bf16[4,4096]{1,0:T(4,128)(2,1)} %param.35) | copy-start | bytes 98308
  54.6 5.8 %copy-start.7 = (bf16[4096]{0:T(1024)(128)(2,1)S(1)}, bf16[4096]{0:T(1024)(128)(2,1)}, u32[]{:S(2)}) copy-start(bf16[4096]{0:T(1024)(128)(2,1)} %param.34) | copy-start | bytes 24580
  54.6 18.7 %copy-start.5 = (bf16[16,2,4096]{2,1,0:T(2,128)(2,1)S(1)}, bf16[16,2,4096]{2,1,0:T(2,128)(2,1)}, u32[]{:S(2)}) copy-start(bf16[16,2,4096]{2,1,0:T(2,128)(2,1)} %param.21) | copy-start | bytes 786436
  60.3 13.1 %copy-start.9 = (bf16[4096]{0:T(1024)(128)(2,1)S(1)}, bf16[4096]{0:T(1024)(128)(2,1)}, u32[]{:S(2)}) copy-start(bf16[4096]{0:T(1024)(128)(2,1)} %param.36) | copy-start | bytes 24580
  60.3 30.2 %copy-start.10 = (s32[64,2,2]{0,2,1:T(2,128)S(1)}, s32[64,2,2]{0,2,1:T(2,128)}, u32[]{:S(2)}) copy-start(s32[64,2,2]{0,2,1:T(2,128)} %param.41) | copy-start | bytes 3076
  60.3 56.9 %copy-start.8 = (bf16[4096,4]{0,1:T(4,128)(2,1)S(1)}, bf16[4096,4]{0,1:T(4,128)(2,1)}, u32[]{:S(2)}) copy-start(bf16[4096,4]{0,1:T(4,128)(2,1)} %param.37) | copy-start | bytes 98308
  60.3 56.9 %all-gather.2.cloned.1.call-start = ((), (), s32[]{:S(2)}) async-start(), calls=%async_computation.3 | async-start | bytes 1310720 | tf_op jit(solution)/shard_map/all_gather | solution.py:461
  90.5 132.2 %reduce-scatter.5.cloned.1.call-start = ((), (), s32[]{:S(2)}) async-start(), calls=%async_computation.4 | async-start | bytes 1310720 | tf_op jit(solution)/shard_map/reduce_scatter | solution.py:468
  194.4 28.2 %copy-start.4 = (bf16[32,4096]{1,0:T(8,128)(2,1)S(1)}, bf16[32,4096]{1,0:T(8,128)(2,1)}, u32[]{:S(2)}) copy-start(bf16[32,4096]{1,0:T(8,128)(2,1)} %reduce-scatter.3.cloned.1.call-done) | copy-start | bytes 786436
Sparse Core Ops, SparseCore 0:
  60.4 27.0 reduce-scatter.2
  90.6 26.5 all-gather.1
  197.5 25.1 reduce-scatter.4

commit v2 on v1

--- a/solution.py
+++ b/solution.py
@@ -19,8 +19,8 @@
 def remove_directions(steering, refusal):
     vector = steering.astype(jnp.float32)
     units = []
-    for k in range(refusal.shape[0]):
-        r = refusal[k].astype(jnp.float32)
+    for direction in refusal:
+        r = direction.astype(jnp.float32)
         for q in units:
             r = r - jnp.sum(q * r) * q
         r = r * lax.rsqrt(jnp.sum(r * r) + EPS)
@@ -28,11 +28,6 @@
     for q in units:
         vector = vector - jnp.sum(q * vector) * q
     return vector
-
-
-def root_mean_normed(residual, norm_gain):
-    scaled = residual * lax.rsqrt(jnp.mean(residual * residual, axis=-1, keepdims=True) + EPS)
-    return (scaled * norm_gain.astype(jnp.float32)).astype(jnp.bfloat16)
 
 
 def owner_weight(normed, router, picked_indices, owner):
@@ -275,14 +270,34 @@
 
 
 def experts_kernel(seq_count, x_ref, gate_ref, up_ref, down_ref, out_ref, pieces, mine, theirs, beside,
-                   arrived, send_x, recv_x, send_f, recv_f, send_p, recv_p, send_o, recv_o):
+                   arrived, relay, send_x, recv_x, send_f, recv_f, send_p, recv_p, send_o, recv_o, send_d,
+                   recv_d, send_e, recv_e, send_g, recv_g):
     chips, chip, core, sibling, ahead = chip_places(seq_count)
+    expert = lax.axis_index("expert")
     cap, d_model = x_ref.shape
+    half = d_model // 2
     chunk = 512
+    square = chips == 4
     greet([sibling] + [ahead(r) for r in range(1, chips)])
 
+    def onward(r):
+        if not square:
+            return ahead(r)
+        other = {1: chip // 2 * 2 + 1 - chip % 2, 2: (chip + 2) % 4, 3: 3 - chip}[r]
+        return (other * 2 + core, expert)
+
+    def homeward(r):
+        return onward(r) if square else ahead(chips - r)
+
+    def halves(k):
+        return pl.ds(k * half, half)
+
     def tokens(r):
-        return push(x_ref, pieces.at[r, 0], send_x, recv_x, r, ahead(r))
+        return push(x_ref, pieces.at[r, 0], send_x, recv_x, r, onward(r))
+
+    def relayed(k):
+        return push(pieces.at[1 + k, 0, :, halves(k)], pieces.at[3, 0, :, halves(k)], send_d, recv_d, k,
+                    onward(2 - k))
 
     def handed(r):
         return push(pieces.at[r, 0], pieces.at[r, 1], send_f, recv_f, r, sibling)
@@ -291,9 +306,16 @@
         return push(theirs.at[r], beside.at[r], send_p, recv_p, r, sibling)
 
     def back(r):
-        return push(mine.at[r], arrived.at[r], send_o, recv_o, r, ahead(chips - r))
-
-    for r in range(1, chips):
+        return push(mine.at[r], arrived.at[r], send_o, recv_o, r, homeward(r))
+
+    def back_first(k):
+        return push(mine.at[3, :, halves(k)], relay.at[k], send_e, recv_e, k, onward(1 + k))
+
+    def back_second(k):
+        return push(relay.at[k], arrived.at[3, :, halves(k)], send_g, recv_g, k, onward(2 - k))
+
+    near = (1, 2) if square else tuple(range(1, chips))
+    for r in near:
         tokens(r).start()
     pieces[0, 0] = x_ref[...]
     handed(0).start()
@@ -316,14 +338,7 @@
         lax.fori_loop(0, d_model // chunk, columns, 0)
         within(r).start()
 
-    handed(0).wait_recv()
-    compute(0)
-
-    def turn(r, _):
-        tokens(r).wait_recv()
-        handed(r).start()
-        handed(r).wait_recv()
-        compute(r)
+    def chip_total(r):
         within(r).wait_recv()
 
         def add(j, _):
@@ -333,29 +348,69 @@
             return 0
 
         lax.fori_loop(0, d_model // chunk, add, 0)
-        back(r).start()
-        return 0
-
-    lax.fori_loop(1, chips, turn, 0)
+
+    handed(0).wait_recv()
+    compute(0)
+    if square:
+        for r in near:
+            tokens(r).wait_recv()
+            relayed(r - 1).start()
+            handed(r).start()
+        for r in near:
+            handed(r).wait_recv()
+            compute(r)
+            chip_total(r)
+            back(r).start()
+        for k in range(2):
+            relayed(k).wait_recv()
+        handed(3).start()
+        handed(3).wait_recv()
+        compute(3)
+        chip_total(3)
+        for k in range(2):
+            back_first(k).start()
+        for k in range(2):
+            back_first(k).wait_recv()
+            back_second(k).start()
+    else:
+
+        def turn(r, _):
+            tokens(r).wait_recv()
+            handed(r).start()
+            handed(r).wait_recv()
+            compute(r)
+            chip_total(r)
+            back(r).start()
+            return 0
+
+        lax.fori_loop(1, chips, turn, 0)
     within(0).wait_recv()
-    for r in range(1, chips):
+    for r in near:
         back(r).wait_recv()
 
     def finish(j, _):
         cols = pl.ds(pl.multiple_of(j * chunk, chunk), chunk)
         total = mine[0, :, cols].astype(jnp.float32) + beside[0, :, cols].astype(jnp.float32)
-        for r in range(1, chips):
+        for r in near:
             total = total + arrived[r, :, cols].astype(jnp.float32)
         out_ref[:, cols] = total
         return 0
 
     lax.fori_loop(0, d_model // chunk, finish, 0)
+    if square:
+        for k in range(2):
+            back_second(k).wait_recv()
+        out_ref[...] = out_ref[...] + arrived[3].astype(jnp.float32)
+        for k in range(2):
+            relayed(k).wait_send()
+            back_first(k).wait_send()
+            back_second(k).wait_send()
     for r in range(chips):
         handed(r).wait_send()
         within(r).wait_send()
-        if r > 0:
-            tokens(r).wait_send()
-            back(r).wait_send()
+    for r in near:
+        tokens(r).wait_send()
+        back(r).wait_send()
 
 
 def run_experts(x, gate, up, down):
@@ -369,12 +424,190 @@
         out_shape=jax.ShapeDtypeStruct((cap, d_model), jnp.float32),
         in_specs=in_vmem(4),
         out_specs=pl.BlockSpec(memory_space=pltpu.VMEM),
-        scratch_shapes=[pltpu.VMEM((chips, 2, cap, d_model), jnp.bfloat16)] + [block] * 4 + [dma] * 8,
+        scratch_shapes=[pltpu.VMEM((chips, 2, cap, d_model), jnp.bfloat16)]
+        + [block] * 4
+        + [pltpu.VMEM((2, cap, d_model // 2), jnp.bfloat16)]
+        + [dma] * 8
+        + [pltpu.SemaphoreType.DMA((2,))] * 6,
         compiler_params=pltpu.CompilerParams(
             collective_id=2, has_side_effects=True, vmem_limit_bytes=60 * 1024 * 1024
         ),
         name="experts",
     )(x, gate, up, down)
+
+
+def line_peers(count):
+    place = lax.axis_index("seq")
+    me = lax.axis_index("expert")
+    return me, [((place, (me + r) % count), (me + r) % count) for r in range(1, count)]
+
+
+def scattered_parts(left_ref, right_ref, part, got, sends, receives, peers, chunks):
+    count = len(peers) + 1
+    rows, d_model = part.shape
+    block = rows // count
+    width = d_model // chunks
+    copies = []
+    for j in range(chunks):
+        cols = pl.ds(j * width, width)
+        part[:, cols] = jnp.dot(
+            left_ref[...], right_ref[:, cols], preferred_element_type=jnp.float32
+        ).astype(jnp.bfloat16)
+        for r, (device, other) in enumerate(peers):
+            at = pl.ds(pl.multiple_of(other * block, block), block)
+            copy = push(part.at[at, cols], got.at[r, :, cols], sends, receives, r * chunks + j, device)
+            copy.start()
+            copies.append(copy)
+    return copies
+
+
+def mix_kernel(count, chunks, gated_ref, proj_ref, input_ref, steer_ref, refusal_ref, gain_ref, residual_ref,
+               normed_ref, part, got, send_a, recv_a, send_r, recv_r, send_l, recv_l):
+    me, peers = line_peers(count)
+    place = lax.axis_index("seq")
+    block = input_ref.shape[0]
+    d_model = input_ref.shape[1]
+    greet([device for device, _ in peers])
+    copies = scattered_parts(gated_ref, proj_ref, part, got, send_a, recv_a, peers, chunks)
+    steering = remove_directions(steer_ref[...], [refusal_ref[k : k + 1, :] for k in range(refusal_ref.shape[0])])
+    mine = pl.ds(pl.multiple_of(me * block, block), block)
+    residual_ref[...] = (
+        input_ref[...].astype(jnp.float32) + steering + part[mine, :].astype(jnp.float32)
+    )
+    for copy in copies:
+        copy.wait_recv()
+    width = d_model // chunks
+    squares = jnp.zeros((block, 1), jnp.float32)
+    for j in range(chunks):
+        cols = pl.ds(j * width, width)
+        total = residual_ref[:, cols]
+        for r in range(count - 1):
+            total = total + got[r, :, cols].astype(jnp.float32)
+        residual_ref[:, cols] = total
+        squares = squares + jnp.sum(total * total, axis=1, keepdims=True)
+    scale = lax.rsqrt(squares / d_model + EPS)
+    for j in range(chunks):
+        cols = pl.ds(j * width, width)
+        normed_ref[mine, cols] = (
+            residual_ref[:, cols] * scale * gain_ref[:, cols].astype(jnp.float32)
+        ).astype(jnp.bfloat16)
+
+    def moved(owner, sends, receives, step, by):
+        at = pl.ds(pl.multiple_of(owner * block, block), block)
+        device = (place, (me + by + count) % count)
+        return push(normed_ref.at[at], normed_ref.at[at], sends, receives, step, device)
+
+    def right(step):
+        return moved((me - step + count) % count, send_r, recv_r, step, 1)
+
+    def left(step):
+        return moved((me + step) % count, send_l, recv_l, step, -1)
+
+    for step in range(count):
+        if step > 0:
+
+            @pl.when(me >= step)
+            def _():
+                right(step - 1).wait_recv()
+
+            @pl.when(me + step < count)
+            def _():
+                left(step - 1).wait_recv()
+
+        if step < count - 1:
+
+            @pl.when((me >= step) & (me + 1 < count))
+            def _():
+                right(step).start()
+
+            @pl.when((me + step < count) & (me > 0))
+            def _():
+                left(step).start()
+
+    for step in range(count - 1):
+
+        @pl.when((me >= step) & (me + 1 < count))
+        def _():
+            right(step).wait_send()
+
+        @pl.when((me + step < count) & (me > 0))
+        def _():
+            left(step).wait_send()
+
+    for copy in copies:
+        copy.wait_send()
+
+
+def mix(gated, out_proj, own_input, steering, refusal, gain):
+    count = lax.axis_size("expert")
+    chunks = 4
+    rows = gated.shape[0]
+    block, d_model = own_input.shape
+    many = pltpu.SemaphoreType.DMA(((count - 1) * chunks,))
+    few = pltpu.SemaphoreType.DMA((count,))
+    return pl.pallas_call(
+        lambda *refs: mix_kernel(count, chunks, *refs),
+        out_shape=[
+            jax.ShapeDtypeStruct((block, d_model), jnp.float32),
+            jax.ShapeDtypeStruct((rows, d_model), jnp.bfloat16),
+        ],
+        in_specs=in_vmem(6),
+        out_specs=in_vmem(2),
+        scratch_shapes=[
+            pltpu.VMEM((rows, d_model), jnp.bfloat16),
+            pltpu.VMEM((count - 1, block, d_model), jnp.bfloat16),
+            many,
+            many,
+        ]
+        + [few] * 4,
+        compiler_params=pltpu.CompilerParams(
+            collective_id=3, has_side_effects=True, vmem_limit_bytes=VMEM_LIMIT
+        ),
+        name="mix",
+    )(gated, out_proj, own_input, steering, refusal, gain)
+
+
+def combine_kernel(count, chunks, spread_ref, weighted_ref, residual_ref, out_ref, part, got, send_a, recv_a):
+    me, peers = line_peers(count)
+    block, d_model = residual_ref.shape
+    greet([device for device, _ in peers])
+    copies = scattered_parts(spread_ref, weighted_ref, part, got, send_a, recv_a, peers, chunks)
+    mine = pl.ds(pl.multiple_of(me * block, block), block)
+    out_ref[...] = residual_ref[...] + part[mine, :].astype(jnp.float32)
+    width = d_model // chunks
+    for copy in copies:
+        copy.wait_recv()
+    for j in range(chunks):
+        cols = pl.ds(j * width, width)
+        total = out_ref[:, cols]
+        for r in range(count - 1):
+            total = total + got[r, :, cols].astype(jnp.float32)
+        out_ref[:, cols] = total
+    for copy in copies:
+        copy.wait_send()
+
+
+def combine(spread, weighted, residual):
+    count = lax.axis_size("expert")
+    chunks = 4
+    block, d_model = residual.shape
+    many = pltpu.SemaphoreType.DMA(((count - 1) * chunks,))
+    return pl.pallas_call(
+        lambda *refs: combine_kernel(count, chunks, *refs),
+        out_shape=jax.ShapeDtypeStruct((block, d_model), jnp.float32),
+        in_specs=in_vmem(3),
+        out_specs=pl.BlockSpec(memory_space=pltpu.VMEM),
+        scratch_shapes=[
+            pltpu.VMEM((block * count, d_model), jnp.bfloat16),
+            pltpu.VMEM((count - 1, block, d_model), jnp.bfloat16),
+            many,
+            many,
+        ],
+        compiler_params=pltpu.CompilerParams(
+            collective_id=4, has_side_effects=True, vmem_limit_bytes=VMEM_LIMIT
+        ),
+        name="combine",
+    )(spread, weighted, residual)
 
 
 def entering_state(totals, states, alog, carry):
@@ -440,8 +673,6 @@
         dtx, actx, alog, bc, entering, d_skip.reshape(groups, LANES), gate_branch.reshape(row_count, channels)
     )
     d_model = out_proj.shape[1]
-    mixed = jnp.dot(gated, out_proj, preferred_element_type=jnp.float32)
-    steering_clean = remove_directions(steering, refusal)
     owner = lax.axis_index("expert")
     own_length = layer_input.shape[0]
     top_count = expert_ids.shape[-1]
@@ -451,22 +682,20 @@
     row_ids = expert_ids.reshape(row_count, top_count)
     slots = slot_matrix(row_ids, owner, capacity)
     slots16 = slots.astype(jnp.bfloat16)
-    own_mixed = lax.psum_scatter(
-        mixed.astype(jnp.bfloat16), "expert", scatter_dimension=0, tiled=True
-    ).astype(jnp.float32)
-    own_residual = (
-        layer_input.astype(jnp.float32).reshape(own_length * prompts, d_model) + own_mixed + steering_clean
+    own_residual, normed = mix(
+        gated,
+        out_proj,
+        layer_input.reshape(own_length * prompts, d_model),
+        steering.reshape(1, d_model),
+        refusal,
+        norm_gain.reshape(1, d_model),
     )
-    own_normed = root_mean_normed(own_residual, norm_gain)
-    normed = lax.all_gather(own_normed, "expert", axis=0, tiled=True)
     weight_rows = owner_weight(normed, router, row_ids, owner)
     expert_in = jnp.dot(slots16, normed, preferred_element_type=jnp.float32).astype(jnp.bfloat16)
     slot_weight = jnp.sum(jnp.where(slots, weight_rows[None, :], 0.0), axis=1)
     expert_out = run_experts(expert_in, specialist_switch_matrix[0], w_up[0], w_down[0])
     weighted = (expert_out * slot_weight[:, None]).astype(jnp.bfloat16)
-    spread = jnp.dot(slots16.T, weighted, preferred_element_type=jnp.float32).astype(jnp.bfloat16)
-    combined = lax.psum_scatter(spread, "expert", scatter_dimension=0, tiled=True)
-    return (own_residual + combined.astype(jnp.float32)).reshape(own_length, prompts, d_model)
+    return combine(slots16.T, weighted, own_residual).reshape(own_length, prompts, d_model)
 
 
 def solution(mesh):

time: 232 us -> 191 us (0.82)
  Pallas kernels: 106 us -> 174 us
  waiting for transfers between devices: 62.8 us -> 0.01 us
  other arithmetic: 24.7 us -> 5.85 us
  between operations: 16.3 us -> 0.41 us
  matrix products: 12.9 us -> 1.94 us
    pallas_call x0 -> x2, Pallas kernels: none -> 77.5 us  [the longest x1 51.3 us: mix(): pl.pallas_call(lambda *refs: mix_kernel(count, chunks, *refs), out_shape=...]
    reduce_scatter x2 -> x0, waiting for transfers between devices: 37 us -> none  [the longest x1 25.3 us: shards(): lax.psum_scatter(spread, 'expert', scatter_dimension=0, tiled=True)]
    all_gather x1 -> x0, waiting for transfers between devices: 25.7 us -> none  [shards(): normed = lax.all_gather(own_normed, 'expert', axis=0, tiled=True)]
    reduce_sum x9 -> x0, other arithmetic: 14.4 us -> none  [the longest x4 7.63 us: remove_directions(): vector = vector - jnp.sum(q * vector) * q]
    pallas_call x1, Pallas kernels: 72.9 us -> 62 us  [run_experts(): pl.pallas_call(lambda *refs: experts_kernel(seq_count, *refs), out_shape=...]
    dot_general x2 -> x0, matrix products: 8.54 us -> none  [the longest x1 5.69 us: shards(): mixed = jnp.dot(gated, out_proj, preferred_element_type=jnp.float32)]
  transfers between devices with their start and end apart: 4 -> 1, of which waited for: 3 -> 0; matrix products, arithmetic and copies ran while one was open for 9% -> 4% of each run, Pallas kernels for 0% -> 0%
where the time goes in v2:
time: 191 us
  Pallas kernels  174 us (91%)
  local copies, waits for them, and re-layouts  6.74 us (4%)
  other arithmetic  5.85 us (3%)
  starting transfers between devices  2.36 us (1%)
  matrix products  1.94 us (1%)
    pallas_call x1, Pallas kernels, run_experts(): pl.pallas_call(lambda *refs: experts_kernel(seq_count, *refs), out_shape=...  62 us
    pallas_call x1, Pallas kernels, mix(): pl.pallas_call(lambda *refs: mix_kernel(count, chunks, *refs), out_shape=...  51.3 us
    pallas_call x1, Pallas kernels, combine(): pl.pallas_call(lambda *refs: combine_kernel(count, chunks, *refs), out_sh...  26.2 us
    pallas_call x1, Pallas kernels, expert_sum(): pl.pallas_call(lambda *refs: expert_sum_kernel(count, *refs), out_shape=j...  15 us
    pallas_call x1, Pallas kernels, state_gather(): pl.pallas_call(lambda *refs: state_gather_kernel(seq_count, *refs), out_s...  11.4 us
    pallas_call x1, Pallas kernels, gated_output(): pl.pallas_call(body, out_shape=jax.ShapeDtypeStruct((rows, channels), jnp...  4.01 us
  transfers between devices with their start and end apart: 1, of which 0 were waited for; matrix products, arithmetic and copies ran while one was open for 4% of the time, Pallas kernels for 0%

profile of v2, /device:TPU:0, one launch (start us, length us, event | category | flops | bytes accessed | tf_op | source)
XLA Modules:
  0.0 191.0 jit_solution(2164802207001015083)
XLA Ops:
  0.0 0.0 copy-start
  0.0 0.0 copy-start.10
  0.0 0.8 slice.115
  0.8 2.4 %collective-permute-start = (bf16[3,2,1024]{2,1,0:T(2,128)(2,1)S(1)}, bf16[3,2,1024]{2,1,0:T(2,128)(2,1)S(1)}, u32[]{:S(2)}, u32[]{:S(2)}) collective-permute-start(bf16[3,2,1024]{2,1,0:T(2,128)(2,1)S(1)} %slice.115), channel_id=1, source_target_pairs={{0,4},{4,8},{8,12},{12,16},{16,20},{20,24},{24,28},{1,5},{5,9},{9,... | collective-permute-start | bytes 36872 | tf_op jit(solution)/shard_map/ppermute | solution.py:16
  3.2 0.7 compare_reduce_fusion
  3.9 0.1 copy.40
  4.0 0.9 slice_convert_fusion.4
  4.9 0.9 copy.44
  5.8 0.1 copy.38
  5.9 0.1 reshape.158
  6.0 0.2 reduce-window.8
  6.1 0.1 add_reduce_fusion
  6.2 0.2 and.17
  6.4 0.1 fusion.15.refs_0_
  6.5 0.8 copy.42
  7.3 0.7 convert_element_type.86
  8.0 0.9 copy.45
  8.9 1.1 reshape.148.refs_6_
  10.0 0.1 reshape.149.refs_2_
  10.1 0.0 copy-done.10
  10.2 0.1 eq.64
  10.3 0.0 collective-permute-done
  10.3 0.0 copy-done.8
  10.4 0.3 maximum_convert_fusion
  10.7 0.9 divide_multiply_fusion
  11.6 0.0 copy-start.1
  11.6 0.0 copy-start.3
  11.6 0.4 reshape.142.refs_3_
  12.0 0.4 fusion.4.refs_0_
  12.4 15.0 %expert_sum.1 = f32[128,288]{1,0:T(8,128)S(1)} custom-call(f32[128,288]{1,0:T(8,128)S(1)} %fusion.4.refs_0_), custom_call_target="tpu_custom_call" | custom-call | tf_op jit(solution)/shard_map/expert_sum/pallas_call | solution.py:218
  27.4 0.1 reshape.145.refs_5_.refs_3_
  27.5 0.0 copy-done.3
  27.5 3.8 %local_states.1 = (f32[1024,128]{1,0:T(8,128)S(1)}, f32[1024,128]{1,0:T(8,128)S(1)}, f32[2,16,8,128]{3,2,1,0:T(8,128)S(1)}, f32[2,8,128]{2,1,0:T(8,128)S(1)}) custom-call(bf16[128,256]{1,0:T(8,128)(2,1)S(1)} %slice.197.refs_0_, bf16[256,1024]{1,0:T(8,128)(2,1)S(1)} %copy-done.1, f32[1,1024]{1,0:T(1,128)S(1)} %bitcast.97, f32[128,1024]{1,0:T(8,128)S(1)} %reshape.142.refs_3_, ...), custom_call_target="tpu_custom_call" | custom-call | tf_op jit(solution)/shard_map/local_states/pallas_call | solution.py:122
  31.3 0.0 copy-start.4
  31.3 11.4 %state_gather.1 = f32[8,2,17,8,128]{4,3,2,1,0:T(8,128)S(1)} custom-call(f32[2,17,8,128]{3,2,1,0:T(8,128)S(1)} %pad_maximum_fusion.refs_0_), custom_call_target="tpu_custom_call" | custom-call | tf_op jit(solution)/shard_map/state_gather/pallas_call | solution.py:259
  42.7 0.0 copy-start.2
  42.8 0.2 fusion.7.refs_4_
  43.0 4.0 %gated_output.1.refs_0_ = bf16[128,1024]{1,0:T(8,128)(2,1)S(1)} custom-call(f32[1024,128]{1,0:T(8,128)S(1)} %get-tuple-element.11.refs_0_, f32[1024,128]{1,0:T(8,128)S(1)} %get-tuple-element.12.refs_1_, f32[16,8,128]{2,1,0:T(8,128)S(1)} %bitcast.95, f32[4096]{0:T(1024)S(1)} %reshape.145.refs_5_.refs_3_, f32[2,16,8,128]{3,2,1,0:T(8,128)S(1)} %fusion.7.refs_4_, ...), custom_call_target="tpu_custom_call" | custom-call | tf_op jit(solution)/shard_map/gated_output/pallas_call | solution.py:142
  47.0 51.3 %mix.1 = (f32[32,4096]{1,0:T(8,128)S(1)}, bf16[128,4096]{1,0:T(8,128)(2,1)S(1)}) custom-call(bf16[128,1024]{1,0:T(8,128)(2,1)S(1)} %gated_output.1.refs_0_, bf16[1024,4096]{1,0:T(8,128)(2,1)} %refs_1_.3, bf16[32,4096]{1,0:T(8,128)(2,1)S(1)} %reshape.149.refs_2_, bf16[1,4096]{1,0:T(2,128)(2,1)S(1)} %reshape.150.refs_3_, bf16[4,4096]{1,0:T(4,128)(2,1)S(1)} %copy-done.2, ...), custom_call_target="tpu_custom_call" | custom-call | tf_op jit(solution)/shard_map/mix/pallas_call | solution.py:548
  98.4 0.0 copy-start.7
  98.4 1.2 convolution_convert_fusion.refs_0_
  99.6 0.4 fusion.20
  100.0 0.1 multiply_reduce_fusion
  100.1 0.1 select_reduce_fusion
  100.3 62.0 %experts.1 = f32[80,4096]{1,0:T(8,128)} custom-call(bf16[80,4096]{1,0:T(8,128)(2,1)} %convolution_convert_fusion.refs_0_, bf16[4096,256]{1,0:T(8,128)(2,1)} %bitcast.99, bf16[4096,256]{1,0:T(8,128)(2,1)} %bitcast.100, bf16[256,4096]{1,0:T(8,128)(2,1)} %bitcast.101), custom_call_target="tpu_custom_call" | custom-call | tf_op jit(solution)/shard_map/experts/pallas_call | solution.py:422
  162.2 1.5 multiply_convert_fusion.refs_1_
  163.7 26.2 %combine.1 = f32[32,4096]{1,0:T(8,128)S(1)} custom-call(bf16[128,80]{1,0:T(8,128)(2,1)S(1)} %fusion.15.refs_0_, bf16[80,4096]{1,0:T(8,128)(2,1)S(1)} %multiply_convert_fusion.refs_1_, f32[32,4096]{1,0:T(8,128)S(1)} %get-tuple-element.16.refs_2_), custom_call_target="tpu_custom_call" | custom-call | tf_op jit(solution)/shard_map/combine/pallas_call | solution.py:595
  189.9 1.1 reshape.152
  (26 shorter events, 0.2 us)
Async XLA Ops:
  0.0 12.0 %copy-start = (bf16[1024,288]{0,1:T(8,128)(2,1)S(1)}, bf16[1024,288]{0,1:T(8,128)(2,1)}, u32[]{:S(2)}) copy-start(bf16[1024,288]{0,1:T(8,128)(2,1)} %param.26) | copy-start | bytes 1769476
  0.0 10.4 %copy-start.5 = (bf16[64,2,1024]{2,1,0:T(2,128)(2,1)S(1)}, bf16[64,2,1024]{2,1,0:T(2,128)(2,1)}, u32[]{:S(2)}) copy-start(bf16[64,2,1024]{2,1,0:T(2,128)(2,1)} %param.22) | copy-start | bytes 786436
  0.0 10.0 %copy-start.6 = (bf16[16,2,4096]{2,1,0:T(2,128)(2,1)S(1)}, bf16[16,2,4096]{2,1,0:T(2,128)(2,1)}, u32[]{:S(2)}) copy-start(bf16[16,2,4096]{2,1,0:T(2,128)(2,1)} %param.21) | copy-start | bytes 786436
  0.0 10.1 %copy-start.9 = (bf16[4096]{0:T(1024)(128)(2,1)S(1)}, bf16[4096]{0:T(1024)(128)(2,1)}, u32[]{:S(2)}) copy-start(bf16[4096]{0:T(1024)(128)(2,1)} %param.34) | copy-start | bytes 24580
  0.0 10.1 %copy-start.10 = (bf16[4096]{0:T(1024)(128)(2,1)S(1)}, bf16[4096]{0:T(1024)(128)(2,1)}, u32[]{:S(2)}) copy-start(bf16[4096]{0:T(1024)(128)(2,1)} %param.36) | copy-start | bytes 24580
  0.0 10.3 %copy-start.8 = (bf16[3,2,1024]{2,1,0:T(2,128)(2,1)S(1)}, bf16[3,2,1024]{2,1,0:T(2,128)(2,1)}, u32[]{:S(2)}) copy-start(bf16[3,2,1024]{2,1,0:T(2,128)(2,1)} %param.32) | copy-start | bytes 36868
  0.8 9.5 %collective-permute-start = (bf16[3,2,1024]{2,1,0:T(2,128)(2,1)S(1)}, bf16[3,2,1024]{2,1,0:T(2,128)(2,1)S(1)}, u32[]{:S(2)}, u32[]{:S(2)}) collective-permute-start(bf16[3,2,1024]{2,1,0:T(2,128)(2,1)S(1)} %slice.115), channel_id=1, source_target_pairs={{0,4},{4,8},{8,12},{12,16},{16,20},{20,24},{24,28},{1,5},{5,9},{9,... | collective-permute-start | bytes 36872 | tf_op jit(solution)/shard_map/ppermute | solution.py:16
  11.6 15.9 %copy-start.1 = (bf16[256,1024]{1,0:T(8,128)(2,1)S(1)}, bf16[256,1024]{1,0:T(8,128)(2,1)}, u32[]{:S(2)}) copy-start(bf16[256,1024]{1,0:T(8,128)(2,1)} %refs_1_.2) | copy-start | bytes 1572868
  11.6 15.9 %copy-start.3 = (f32[1024]{0:T(1024)S(1)}, f32[1024]{0:T(1024)}, u32[]{:S(2)}) copy-start(f32[1024]{0:T(1024)} %param.28) | copy-start | bytes 12292
  31.3 11.7 %copy-start.4 = (f32[1024]{0:T(1024)S(1)}, f32[1024]{0:T(1024)}, u32[]{:S(2)}) copy-start(f32[1024]{0:T(1024)} %param.30) | copy-start | bytes 12292
  42.7 4.3 %copy-start.2 = (bf16[4,4096]{1,0:T(4,128)(2,1)S(1)}, bf16[4,4096]{1,0:T(4,128)(2,1)}, u32[]{:S(2)}) copy-start(bf16[4,4096]{1,0:T(4,128)(2,1)} %refs_4_.1) | copy-start | bytes 98308
  98.4 1.2 copy-start.7

commit v3 on v2

--- a/solution.py
+++ b/solution.py
@@ -269,16 +269,19 @@
     )(part)
 
 
-def experts_kernel(seq_count, x_ref, gate_ref, up_ref, down_ref, out_ref, pieces, mine, theirs, beside,
-                   arrived, relay, send_x, recv_x, send_f, recv_f, send_p, recv_p, send_o, recv_o, send_d,
-                   recv_d, send_e, recv_e, send_g, recv_g):
+def experts_kernel(seq_count, count, chunks, x_ref, gate_ref, up_ref, down_ref, spread_ref, weight_ref,
+                   residual_ref, out_ref, pieces, hidden, mine, theirs, beside, arrived, relay, part, got,
+                   send_x, recv_x, send_f, recv_f, send_p, recv_p, send_o, recv_o, send_d, recv_d, send_e,
+                   recv_e, send_g, recv_g, send_z, recv_z):
     chips, chip, core, sibling, ahead = chip_places(seq_count)
     expert = lax.axis_index("expert")
+    me, peers = line_peers(count)
     cap, d_model = x_ref.shape
+    block = residual_ref.shape[0]
     half = d_model // 2
-    chunk = 512
+    width = d_model // chunks
     square = chips == 4
-    greet([sibling] + [ahead(r) for r in range(1, chips)])
+    greet([sibling] + [ahead(r) for r in range(1, chips)] + [device for device, _ in peers])
 
     def onward(r):
         if not square:
@@ -289,30 +292,35 @@
     def homeward(r):
         return onward(r) if square else ahead(chips - r)
 
-    def halves(k):
-        return pl.ds(k * half, half)
-
     def tokens(r):
         return push(x_ref, pieces.at[r, 0], send_x, recv_x, r, onward(r))
 
     def relayed(k):
-        return push(pieces.at[1 + k, 0, :, halves(k)], pieces.at[3, 0, :, halves(k)], send_d, recv_d, k,
-                    onward(2 - k))
+        cols = pl.ds(k * half, half)
+        return push(pieces.at[1 + k, 0, :, cols], pieces.at[3, 0, :, cols], send_d, recv_d, k, onward(2 - k))
 
     def handed(r):
         return push(pieces.at[r, 0], pieces.at[r, 1], send_f, recv_f, r, sibling)
 
-    def within(r):
-        return push(theirs.at[r], beside.at[r], send_p, recv_p, r, sibling)
-
-    def back(r):
-        return push(mine.at[r], arrived.at[r], send_o, recv_o, r, homeward(r))
-
-    def back_first(k):
-        return push(mine.at[3, :, halves(k)], relay.at[k], send_e, recv_e, k, onward(1 + k))
-
-    def back_second(k):
-        return push(relay.at[k], arrived.at[3, :, halves(k)], send_g, recv_g, k, onward(2 - k))
+    def within(j):
+        return push(theirs.at[j], beside.at[j], send_p, recv_p, j, sibling)
+
+    def back(j, r):
+        return push(mine.at[j, r], arrived.at[j, r], send_o, recv_o, j * chips + r, homeward(r))
+
+    def back_first(j, k):
+        cols = pl.ds(k * (width // 2), width // 2)
+        return push(mine.at[j, 3, :, cols], relay.at[j, k], send_e, recv_e, j * 2 + k, onward(1 + k))
+
+    def back_second(j, k):
+        cols = pl.ds(k * (width // 2), width // 2)
+        return push(relay.at[j, k], arrived.at[j, 3, :, cols], send_g, recv_g, j * 2 + k, onward(2 - k))
+
+    def outward(j, r):
+        device, other = peers[r]
+        cols = pl.ds(j * width, width)
+        at = pl.ds(pl.multiple_of(other * block, block), block)
+        return push(part.at[at, cols], got.at[r, :, cols], send_z, recv_z, j * (count - 1) + r, device)
 
     near = (1, 2) if square else tuple(range(1, chips))
     for r in near:
@@ -324,30 +332,9 @@
         rows = pieces[r].reshape(2 * cap, d_model)
         gate = jnp.dot(rows, gate_ref[...], preferred_element_type=jnp.float32)
         upward = jnp.dot(rows, up_ref[...], preferred_element_type=jnp.float32)
-        hidden = (gate * jax.nn.sigmoid(gate) * upward).astype(jnp.bfloat16)
-
-        def columns(j, _):
-            cols = pl.ds(pl.multiple_of(j * chunk, chunk), chunk)
-            part = jnp.dot(hidden, down_ref[:, cols], preferred_element_type=jnp.float32).astype(
-                jnp.bfloat16
-            )
-            mine[r, :, cols] = part[:cap]
-            theirs[r, :, cols] = part[cap:]
-            return 0
-
-        lax.fori_loop(0, d_model // chunk, columns, 0)
-        within(r).start()
-
-    def chip_total(r):
-        within(r).wait_recv()
-
-        def add(j, _):
-            cols = pl.ds(pl.multiple_of(j * chunk, chunk), chunk)
-            total = mine[r, :, cols].astype(jnp.float32) + beside[r, :, cols].astype(jnp.float32)
-            mine[r, :, cols] = total.astype(jnp.bfloat16)
-            return 0
-
-        lax.fori_loop(0, d_model // chunk, add, 0)
+        fresh = (gate * jax.nn.sigmoid(gate) * upward).astype(jnp.bfloat16)
+        hidden[0, r] = fresh[:cap]
+        hidden[1, r] = fresh[cap:]
 
     handed(0).wait_recv()
     compute(0)
@@ -359,19 +346,11 @@
         for r in near:
             handed(r).wait_recv()
             compute(r)
-            chip_total(r)
-            back(r).start()
         for k in range(2):
             relayed(k).wait_recv()
         handed(3).start()
         handed(3).wait_recv()
         compute(3)
-        chip_total(3)
-        for k in range(2):
-            back_first(k).start()
-        for k in range(2):
-            back_first(k).wait_recv()
-            back_second(k).start()
     else:
 
         def turn(r, _):
@@ -379,61 +358,141 @@
             handed(r).start()
             handed(r).wait_recv()
             compute(r)
-            chip_total(r)
-            back(r).start()
             return 0
 
         lax.fori_loop(1, chips, turn, 0)
-    within(0).wait_recv()
-    for r in near:
-        back(r).wait_recv()
-
-    def finish(j, _):
-        cols = pl.ds(pl.multiple_of(j * chunk, chunk), chunk)
-        total = mine[0, :, cols].astype(jnp.float32) + beside[0, :, cols].astype(jnp.float32)
+
+    def project(j):
+        cols = pl.ds(j * width, width)
+        for side, target in ((1, theirs), (0, mine)):
+
+            def one(r, _):
+                target[j, r] = jnp.dot(
+                    hidden[side, r], down_ref[:, cols], preferred_element_type=jnp.float32
+                ).astype(jnp.bfloat16)
+                return 0
+
+            if square:
+                rows = hidden[side].reshape(chips * cap, hidden.shape[-1])
+                target[j] = (
+                    jnp.dot(rows, down_ref[:, cols], preferred_element_type=jnp.float32)
+                    .astype(jnp.bfloat16)
+                    .reshape(chips, cap, width)
+                )
+            else:
+                lax.fori_loop(0, chips, one, 0)
+            if side == 1:
+                within(j).start()
+
+    def chip_total(j):
+        within(j).wait_recv()
+
+        def add(r, _):
+            total = mine[j, r].astype(jnp.float32) + beside[j, r].astype(jnp.float32)
+            mine[j, r] = total.astype(jnp.bfloat16)
+            return 0
+
+        lax.fori_loop(1, chips, add, 0)
+        if square:
+            for k in range(2):
+                back_first(j, k).start()
         for r in near:
-            total = total + arrived[r, :, cols].astype(jnp.float32)
+            back(j, r).start()
+
+    def pass_on(j):
+        if square:
+            for k in range(2):
+                back_first(j, k).wait_recv()
+                back_second(j, k).start()
+
+    def go_home(j):
+        cols = pl.ds(j * width, width)
+        total = mine[j, 0].astype(jnp.float32) + beside[j, 0].astype(jnp.float32)
+        for r in near:
+            back(j, r).wait_recv()
+            total = total + arrived[j, r].astype(jnp.float32)
+        if square:
+            for k in range(2):
+                back_second(j, k).wait_recv()
+            total = total + arrived[j, 3].astype(jnp.float32)
+        weighted = (total * weight_ref[...]).astype(jnp.bfloat16)
+        part[:, cols] = jnp.dot(spread_ref[...], weighted, preferred_element_type=jnp.float32).astype(
+            jnp.bfloat16
+        )
+        for r in range(count - 1):
+            outward(j, r).start()
+
+    for j in range(chunks + 3):
+        if j < chunks:
+            project(j)
+        if 1 <= j <= chunks:
+            chip_total(j - 1)
+        if 2 <= j <= chunks + 1:
+            pass_on(j - 2)
+        if j >= 3:
+            go_home(j - 3)
+
+    at_home = pl.ds(pl.multiple_of(me * block, block), block)
+    for j in range(chunks):
+        cols = pl.ds(j * width, width)
+        total = residual_ref[:, cols] + part[at_home, cols].astype(jnp.float32)
+        for r in range(count - 1):
+            outward(j, r).wait_recv()
+            total = total + got[r, :, cols].astype(jnp.float32)
         out_ref[:, cols] = total
-        return 0
-
-    lax.fori_loop(0, d_model // chunk, finish, 0)
+
+    for j in range(chunks):
+        within(j).wait_send()
+        for r in near:
+            back(j, r).wait_send()
+        for r in range(count - 1):
+            outward(j, r).wait_send()
+        if square:
+            for k in range(2):
+                back_first(j, k).wait_send()
+                back_second(j, k).wait_send()
     if square:
         for k in range(2):
-            back_second(k).wait_recv()
-        out_ref[...] = out_ref[...] + arrived[3].astype(jnp.float32)
-        for k in range(2):
             relayed(k).wait_send()
-            back_first(k).wait_send()
-            back_second(k).wait_send()
     for r in range(chips):
         handed(r).wait_send()
-        within(r).wait_send()
     for r in near:
         tokens(r).wait_send()
-        back(r).wait_send()
-
-
-def run_experts(x, gate, up, down):
+
+
+def run_experts(x, gate, up, down, spread, weight, residual):
     seq_count = lax.axis_size("seq")
+    count = lax.axis_size("expert")
     chips = seq_count // 2
+    chunks = 4
     cap, d_model = x.shape
-    dma = pltpu.SemaphoreType.DMA((chips,))
-    block = pltpu.VMEM((chips, cap, d_model), jnp.bfloat16)
+    ff = gate.shape[1]
+    block = residual.shape[0]
+    width = d_model // chunks
+    bf16 = jnp.bfloat16
+
+    def pair(many):
+        return [pltpu.SemaphoreType.DMA((many,))] * 2
+
     return pl.pallas_call(
-        lambda *refs: experts_kernel(seq_count, *refs),
-        out_shape=jax.ShapeDtypeStruct((cap, d_model), jnp.float32),
-        in_specs=in_vmem(4),
+        lambda *refs: experts_kernel(seq_count, count, chunks, *refs),
+        out_shape=jax.ShapeDtypeStruct((block, d_model), jnp.float32),
+        in_specs=in_vmem(7),
         out_specs=pl.BlockSpec(memory_space=pltpu.VMEM),
-        scratch_shapes=[pltpu.VMEM((chips, 2, cap, d_model), jnp.bfloat16)]
-        + [block] * 4
-        + [pltpu.VMEM((2, cap, d_model // 2), jnp.bfloat16)]
-        + [dma] * 8
-        + [pltpu.SemaphoreType.DMA((2,))] * 6,
+        scratch_shapes=[pltpu.VMEM((chips, 2, cap, d_model), bf16), pltpu.VMEM((2, chips, cap, ff), bf16)]
+        + [pltpu.VMEM((chunks, chips, cap, width), bf16)] * 4
+        + [
+            pltpu.VMEM((chunks, 2, cap, width // 2), bf16),
+            pltpu.VMEM((count * block, d_model), bf16),
+            pltpu.VMEM((count - 1, block, d_model), bf16),
+        ]
+        + pair(chips) + pair(chips) + pair(chunks) + pair(chunks * chips) + pair(2)
+        + pair(chunks * 2) + pair(chunks * 2) + pair(chunks * (count - 1)),
         compiler_params=pltpu.CompilerParams(
             collective_id=2, has_side_effects=True, vmem_limit_bytes=60 * 1024 * 1024
         ),
         name="experts",
-    )(x, gate, up, down)
+    )(x, gate, up, down, spread, weight, residual)
 
 
 def line_peers(count):
@@ -565,49 +624,6 @@
         ),
         name="mix",
     )(gated, out_proj, own_input, steering, refusal, gain)
-
-
-def combine_kernel(count, chunks, spread_ref, weighted_ref, residual_ref, out_ref, part, got, send_a, recv_a):
-    me, peers = line_peers(count)
-    block, d_model = residual_ref.shape
-    greet([device for device, _ in peers])
-    copies = scattered_parts(spread_ref, weighted_ref, part, got, send_a, recv_a, peers, chunks)
-    mine = pl.ds(pl.multiple_of(me * block, block), block)
-    out_ref[...] = residual_ref[...] + part[mine, :].astype(jnp.float32)
-    width = d_model // chunks
-    for copy in copies:
-        copy.wait_recv()
-    for j in range(chunks):
-        cols = pl.ds(j * width, width)
-        total = out_ref[:, cols]
-        for r in range(count - 1):
-            total = total + got[r, :, cols].astype(jnp.float32)
-        out_ref[:, cols] = total
-    for copy in copies:
-        copy.wait_send()
-
-
-def combine(spread, weighted, residual):
-    count = lax.axis_size("expert")
-    chunks = 4
-    block, d_model = residual.shape
-    many = pltpu.SemaphoreType.DMA(((count - 1) * chunks,))
-    return pl.pallas_call(
-        lambda *refs: combine_kernel(count, chunks, *refs),
-        out_shape=jax.ShapeDtypeStruct((block, d_model), jnp.float32),
-        in_specs=in_vmem(3),
-        out_specs=pl.BlockSpec(memory_space=pltpu.VMEM),
-        scratch_shapes=[
-            pltpu.VMEM((block * count, d_model), jnp.bfloat16),
-            pltpu.VMEM((count - 1, block, d_model), jnp.bfloat16),
-            many,
-            many,
-        ],
-        compiler_params=pltpu.CompilerParams(
-            collective_id=4, has_side_effects=True, vmem_limit_bytes=VMEM_LIMIT
-        ),
-        name="combine",
-    )(spread, weighted, residual)
 
 
 def entering_state(totals, states, alog, carry):
@@ -693,9 +709,16 @@
     weight_rows = owner_weight(normed, router, row_ids, owner)
     expert_in = jnp.dot(slots16, normed, preferred_element_type=jnp.float32).astype(jnp.bfloat16)
     slot_weight = jnp.sum(jnp.where(slots, weight_rows[None, :], 0.0), axis=1)
-    expert_out = run_experts(expert_in, specialist_switch_matrix[0], w_up[0], w_down[0])
-    weighted = (expert_out * slot_weight[:, None]).astype(jnp.bfloat16)
-    return combine(slots16.T, weighted, own_residual).reshape(own_length, prompts, d_model)
+    out = run_experts(
+        expert_in,
+        specialist_switch_matrix[0],
+        w_up[0],
+        w_down[0],
+        slots16.T,
+        slot_weight[:, None],
+        own_residual,
+    )
+    return out.reshape(own_length, prompts, d_model)
 
 
 def solution(mesh):

time: 191 us -> 177 us (0.927)
  Pallas kernels: 174 us -> 157 us
  local copies, waits for them, and re-layouts: 6.74 us -> 9.44 us
    pallas_call x2 -> x1, Pallas kernels: 88.2 us -> 71.7 us  [run_experts(): pl.pallas_call(lambda *refs: experts_kernel(seq_count, count, chunks, *re...]
  transfers between devices with their start and end apart: 1 -> 1, of which waited for: 0 -> 0; matrix products, arithmetic and copies ran while one was open for 4% -> 5% of each run, Pallas kernels for 0% -> 0%
where the time goes in v3:
time: 177 us; the launch traced here: 176 us
  Pallas kernels  157 us (89%)
  local copies, waits for them, and re-layouts  9.44 us (5%)
  other arithmetic  5.01 us (3%)
  starting transfers between devices  2.36 us (1%)
  matrix products  1.9 us (1%)
    pallas_call x1, Pallas kernels, run_experts(): pl.pallas_call(lambda *refs: experts_kernel(seq_count, count, chunks, *re...  71.7 us
    pallas_call x1, Pallas kernels, mix(): pl.pallas_call(lambda *refs: mix_kernel(count, chunks, *refs), out_shape=...  51.4 us
    pallas_call x1, Pallas kernels, expert_sum(): pl.pallas_call(lambda *refs: expert_sum_kernel(count, *refs), out_shape=j...  15 us
    pallas_call x1, Pallas kernels, state_gather(): pl.pallas_call(lambda *refs: state_gather_kernel(seq_count, *refs), out_s...  11.4 us
    pallas_call x1, Pallas kernels, gated_output(): pl.pallas_call(body, out_shape=jax.ShapeDtypeStruct((rows, channels), jnp...  4.01 us
    pallas_call x1, Pallas kernels, local_states(): pl.pallas_call(body, out_shape=[jax.ShapeDtypeStruct((rows * groups, LANE...  3.78 us
  transfers between devices with their start and end apart: 1, of which 0 were waited for; matrix products, arithmetic and copies ran while one was open for 5% of the time, Pallas kernels for 0%

profile of v3, /device:TPU:0, one launch (start us, length us, event | category | flops | bytes accessed | tf_op | source)
XLA Modules:
  0.0 176.3 jit_solution(6297460553020064102)
XLA Ops:
  0.0 0.0 copy-start
  0.0 0.0 copy-start.8
  0.0 0.8 slice.115
  0.8 2.4 %collective-permute-start = (bf16[3,2,1024]{2,1,0:T(2,128)(2,1)S(1)}, bf16[3,2,1024]{2,1,0:T(2,128)(2,1)S(1)}, u32[]{:S(2)}, u32[]{:S(2)}) collective-permute-start(bf16[3,2,1024]{2,1,0:T(2,128)(2,1)S(1)} %slice.115), channel_id=1, source_target_pairs={{0,4},{4,8},{8,12},{12,16},{16,20},{20,24},{24,28},{1,5},{5,9},{9,... | collective-permute-start | bytes 36872 | tf_op jit(solution)/shard_map/ppermute | solution.py:16
  3.2 0.7 compare_reduce_fusion
  3.9 0.1 copy.43
  4.0 0.9 slice_convert_fusion.4
  4.9 0.9 copy.48
  5.8 0.1 copy.41
  5.9 0.1 reshape.157
  5.9 0.2 reduce-window.8
  6.1 0.1 add_reduce_fusion
  6.2 0.2 and.17
  6.4 0.7 fusion.15.refs_4_
  7.1 0.8 copy.45
  7.9 0.7 convert_element_type.82
  8.6 0.9 copy.49
  9.5 1.1 reshape.147.refs_6_
  10.6 1.1 reshape.148.refs_2_
  11.7 0.1 eq.64
  11.8 0.0 collective-permute-done
  11.9 0.0 copy-done.6
  11.9 0.3 maximum_convert_fusion
  12.2 0.9 divide_multiply_fusion
  13.1 0.0 copy-start.2
  13.1 0.0 copy-start.4
  13.1 0.4 reshape.141.refs_3_
  13.5 0.0 copy-done
  13.5 0.4 fusion.4.refs_0_
  13.9 15.0 %expert_sum.1 = f32[128,288]{1,0:T(8,128)S(1)} custom-call(f32[128,288]{1,0:T(8,128)S(1)} %fusion.4.refs_0_), custom_call_target="tpu_custom_call" | custom-call | tf_op jit(solution)/shard_map/expert_sum/pallas_call | solution.py:218
  28.9 0.1 reshape.144.refs_5_.refs_3_
  29.0 0.0 copy-start.5
  29.0 3.8 %local_states.1 = (f32[1024,128]{1,0:T(8,128)S(1)}, f32[1024,128]{1,0:T(8,128)S(1)}, f32[2,16,8,128]{3,2,1,0:T(8,128)S(1)}, f32[2,8,128]{2,1,0:T(8,128)S(1)}) custom-call(bf16[128,256]{1,0:T(8,128)(2,1)S(1)} %slice.197.refs_0_, bf16[256,1024]{1,0:T(8,128)(2,1)S(1)} %copy-done.2, f32[1,1024]{1,0:T(1,128)S(1)} %bitcast.98, f32[128,1024]{1,0:T(8,128)S(1)} %reshape.141.refs_3_, ...), custom_call_target="tpu_custom_call" | custom-call | tf_op jit(solution)/shard_map/local_states/pallas_call | solution.py:122
  32.8 0.0 copy-start.3
  32.8 11.4 %state_gather.1 = f32[8,2,17,8,128]{4,3,2,1,0:T(8,128)S(1)} custom-call(f32[2,17,8,128]{3,2,1,0:T(8,128)S(1)} %pad_maximum_fusion.refs_0_), custom_call_target="tpu_custom_call" | custom-call | tf_op jit(solution)/shard_map/state_gather/pallas_call | solution.py:259
  44.3 0.2 fusion.7.refs_4_
  44.5 4.0 %gated_output.1.refs_0_ = bf16[128,1024]{1,0:T(8,128)(2,1)S(1)} custom-call(f32[1024,128]{1,0:T(8,128)S(1)} %get-tuple-element.11.refs_0_, f32[1024,128]{1,0:T(8,128)S(1)} %get-tuple-element.12.refs_1_, f32[16,8,128]{2,1,0:T(8,128)S(1)} %bitcast.96, f32[4096]{0:T(1024)S(1)} %reshape.144.refs_5_.refs_3_, f32[2,16,8,128]{3,2,1,0:T(8,128)S(1)} %fusion.7.refs_4_, ...), custom_call_target="tpu_custom_call" | custom-call | tf_op jit(solution)/shard_map/gated_output/pallas_call | solution.py:142
  48.5 0.0 copy-start.7
  48.5 51.4 %mix.1 = (f32[32,4096]{1,0:T(8,128)S(1)}, bf16[128,4096]{1,0:T(8,128)(2,1)S(1)}) custom-call(bf16[128,1024]{1,0:T(8,128)(2,1)S(1)} %gated_output.1.refs_0_, bf16[1024,4096]{1,0:T(8,128)(2,1)} %refs_1_.3, bf16[32,4096]{1,0:T(8,128)(2,1)S(1)} %reshape.148.refs_2_, bf16[1,4096]{1,0:T(2,128)(2,1)S(1)} %reshape.149.refs_3_, bf16[4,4096]{1,0:T(4,128)(2,1)S(1)} %copy-done.3, ...), custom_call_target="tpu_custom_call" | custom-call | tf_op jit(solution)/shard_map/mix/pallas_call | solution.py:607
  99.9 0.0 copy-start.1
  99.9 1.2 convolution_convert_fusion.refs_0_
  101.1 0.4 fusion.20
  101.5 0.0 copy-done.1
  101.6 0.1 multiply_reduce_fusion
  101.7 0.1 select_reduce_fusion
  101.8 0.7 copy.46.refs_5_
  102.5 71.7 %experts.1 = f32[32,4096]{1,0:T(8,128)} custom-call(bf16[80,4096]{1,0:T(8,128)(2,1)} %convolution_convert_fusion.refs_0_, bf16[4096,256]{1,0:T(8,128)(2,1)} %bitcast.100, bf16[4096,256]{1,0:T(8,128)(2,1)} %bitcast.101, bf16[256,4096]{1,0:T(8,128)(2,1)} %bitcast.102, bf16[128,80]{1,0:T(8,128)(2,1)} %fusion.15.refs_4_, f32[80,1]{1,0:T(8,128)} %copy.46.refs_5_, ...), custom_call_target="tpu_custom_call" | custom-call | tf_op jit(solution)/shard_map/experts/pallas_call | solution.py:477
  174.2 2.1 %reshape.151 = f32[16,2,4096]{2,1,0:T(2,128)} reshape(f32[32,4096]{1,0:T(8,128)} %experts.1) | data formatting | bytes 1048576 | tf_op jit(solution)/shard_map/reshape | solution.py:721
  (25 shorter events, 0.2 us)
Async XLA Ops:
  0.0 13.5 %copy-start = (bf16[1024,288]{0,1:T(8,128)(2,1)S(1)}, bf16[1024,288]{0,1:T(8,128)(2,1)}, u32[]{:S(2)}) copy-start(bf16[1024,288]{0,1:T(8,128)(2,1)} %param.26) | copy-start | bytes 1769476
  0.0 11.9 %copy-start.6 = (bf16[64,2,1024]{2,1,0:T(2,128)(2,1)S(1)}, bf16[64,2,1024]{2,1,0:T(2,128)(2,1)}, u32[]{:S(2)}) copy-start(bf16[64,2,1024]{2,1,0:T(2,128)(2,1)} %param.22) | copy-start | bytes 786436
  0.0 11.6 %copy-start.9 = (bf16[4096]{0:T(1024)(128)(2,1)S(1)}, bf16[4096]{0:T(1024)(128)(2,1)}, u32[]{:S(2)}) copy-start(bf16[4096]{0:T(1024)(128)(2,1)} %param.34) | copy-start | bytes 24580
  0.0 11.6 %copy-start.10 = (bf16[4096]{0:T(1024)(128)(2,1)S(1)}, bf16[4096]{0:T(1024)(128)(2,1)}, u32[]{:S(2)}) copy-start(bf16[4096]{0:T(1024)(128)(2,1)} %param.36) | copy-start | bytes 24580
  0.0 11.8 %copy-start.8 = (bf16[3,2,1024]{2,1,0:T(2,128)(2,1)S(1)}, bf16[3,2,1024]{2,1,0:T(2,128)(2,1)}, u32[]{:S(2)}) copy-start(bf16[3,2,1024]{2,1,0:T(2,128)(2,1)} %param.32) | copy-start | bytes 36868
  0.8 11.0 %collective-permute-start = (bf16[3,2,1024]{2,1,0:T(2,128)(2,1)S(1)}, bf16[3,2,1024]{2,1,0:T(2,128)(2,1)S(1)}, u32[]{:S(2)}, u32[]{:S(2)}) collective-permute-start(bf16[3,2,1024]{2,1,0:T(2,128)(2,1)S(1)} %slice.115), channel_id=1, source_target_pairs={{0,4},{4,8},{8,12},{12,16},{16,20},{20,24},{24,28},{1,5},{5,9},{9,... | collective-permute-start | bytes 36872 | tf_op jit(solution)/shard_map/ppermute | solution.py:16
  13.1 15.9 %copy-start.2 = (bf16[256,1024]{1,0:T(8,128)(2,1)S(1)}, bf16[256,1024]{1,0:T(8,128)(2,1)}, u32[]{:S(2)}) copy-start(bf16[256,1024]{1,0:T(8,128)(2,1)} %refs_1_.2) | copy-start | bytes 1572868
  13.1 15.9 %copy-start.4 = (f32[1024]{0:T(1024)S(1)}, f32[1024]{0:T(1024)}, u32[]{:S(2)}) copy-start(f32[1024]{0:T(1024)} %param.28) | copy-start | bytes 12292
  29.0 15.5 %copy-start.5 = (f32[1024]{0:T(1024)S(1)}, f32[1024]{0:T(1024)}, u32[]{:S(2)}) copy-start(f32[1024]{0:T(1024)} %param.30) | copy-start | bytes 12292
  32.8 15.7 %copy-start.3 = (bf16[4,4096]{1,0:T(4,128)(2,1)S(1)}, bf16[4,4096]{1,0:T(4,128)(2,1)}, u32[]{:S(2)}) copy-start(bf16[4,4096]{1,0:T(4,128)(2,1)} %refs_4_.1) | copy-start | bytes 98308
  48.5 52.6 %copy-start.7 = (bf16[4096,4]{0,1:T(4,128)(2,1)S(1)}, bf16[4096,4]{0,1:T(4,128)(2,1)}, u32[]{:S(2)}) copy-start(bf16[4096,4]{0,1:T(4,128)(2,1)} %param.37) | copy-start | bytes 98308
  99.9 1.5 copy-start.1

commit v4 on v3

--- a/solution.py
+++ b/solution.py
@@ -464,7 +464,7 @@
     seq_count = lax.axis_size("seq")
     count = lax.axis_size("expert")
     chips = seq_count // 2
-    chunks = 4
+    chunks = 8
     cap, d_model = x.shape
     ff = gate.shape[1]
     block = residual.shape[0]

time: 177 us -> 174 us (0.983)
  Pallas kernels: 157 us -> 155 us
    pallas_call x1, Pallas kernels: 71.7 us -> 69 us  [run_experts(): pl.pallas_call(lambda *refs: experts_kernel(seq_count, count, chunks, *re...]
where the time goes in v4:
time: 174 us
  Pallas kernels  155 us (89%)
  local copies, waits for them, and re-layouts  9.44 us (5%)
  other arithmetic  5.01 us (3%)
  starting transfers between devices  2.36 us (1%)
  matrix products  1.9 us (1%)
    pallas_call x1, Pallas kernels, run_experts(): pl.pallas_call(lambda *refs: experts_kernel(seq_count, count, chunks, *re...  69 us
    pallas_call x1, Pallas kernels, mix(): pl.pallas_call(lambda *refs: mix_kernel(count, chunks, *refs), out_shape=...  51.4 us
    pallas_call x1, Pallas kernels, expert_sum(): pl.pallas_call(lambda *refs: expert_sum_kernel(count, *refs), out_shape=j...  15 us
    pallas_call x1, Pallas kernels, state_gather(): pl.pallas_call(lambda *refs: state_gather_kernel(seq_count, *refs), out_s...  11.4 us
    pallas_call x1, Pallas kernels, gated_output(): pl.pallas_call(body, out_shape=jax.ShapeDtypeStruct((rows, channels), jnp...  4.01 us
    pallas_call x1, Pallas kernels, local_states(): pl.pallas_call(body, out_shape=[jax.ShapeDtypeStruct((rows * groups, LANE...  3.78 us
  transfers between devices with their start and end apart: 1, of which 0 were waited for; matrix products, arithmetic and copies ran while one was open for 5% of the time, Pallas kernels for 0%

profile of v4, /device:TPU:0, one launch (start us, length us, event | category | flops | bytes accessed | tf_op | source)
XLA Modules:
  0.0 173.6 jit_solution(6349101103028964651)
XLA Ops:
  0.0 0.0 copy-start
  0.0 0.0 copy-start.8
  0.0 0.8 slice.115
  0.8 2.4 %collective-permute-start = (bf16[3,2,1024]{2,1,0:T(2,128)(2,1)S(1)}, bf16[3,2,1024]{2,1,0:T(2,128)(2,1)S(1)}, u32[]{:S(2)}, u32[]{:S(2)}) collective-permute-start(bf16[3,2,1024]{2,1,0:T(2,128)(2,1)S(1)} %slice.115), channel_id=1, source_target_pairs={{0,4},{4,8},{8,12},{12,16},{16,20},{20,24},{24,28},{1,5},{5,9},{9,... | collective-permute-start | bytes 36872 | tf_op jit(solution)/shard_map/ppermute | solution.py:16
  3.2 0.7 compare_reduce_fusion
  3.9 0.1 copy.43
  4.0 0.9 slice_convert_fusion.4
  4.9 0.9 copy.48
  5.8 0.1 copy.41
  5.9 0.1 reshape.157
  5.9 0.2 reduce-window.8
  6.1 0.1 add_reduce_fusion
  6.2 0.2 and.17
  6.4 0.7 fusion.15.refs_4_
  7.1 0.8 copy.45
  7.9 0.7 convert_element_type.82
  8.6 0.9 copy.49
  9.5 1.1 reshape.147.refs_6_
  10.6 1.1 reshape.148.refs_2_
  11.6 0.0 copy-done.9
  11.6 0.0 copy-done.10
  11.7 0.1 eq.64
  11.8 0.0 collective-permute-done
  11.8 0.0 copy-done.8
  11.9 0.3 maximum_convert_fusion
  12.2 0.9 divide_multiply_fusion
  13.1 0.0 copy-start.2
  13.1 0.0 copy-start.4
  13.1 0.4 reshape.141.refs_3_
  13.5 0.4 fusion.4.refs_0_
  13.9 15.0 %expert_sum.1 = f32[128,288]{1,0:T(8,128)S(1)} custom-call(f32[128,288]{1,0:T(8,128)S(1)} %fusion.4.refs_0_), custom_call_target="tpu_custom_call" | custom-call | tf_op jit(solution)/shard_map/expert_sum/pallas_call | solution.py:218
  28.9 0.1 reshape.144.refs_5_.refs_3_
  29.0 0.0 copy-start.5
  29.0 3.8 %local_states.1 = (f32[1024,128]{1,0:T(8,128)S(1)}, f32[1024,128]{1,0:T(8,128)S(1)}, f32[2,16,8,128]{3,2,1,0:T(8,128)S(1)}, f32[2,8,128]{2,1,0:T(8,128)S(1)}) custom-call(bf16[128,256]{1,0:T(8,128)(2,1)S(1)} %slice.197.refs_0_, bf16[256,1024]{1,0:T(8,128)(2,1)S(1)} %copy-done.2, f32[1,1024]{1,0:T(1,128)S(1)} %bitcast.98, f32[128,1024]{1,0:T(8,128)S(1)} %reshape.141.refs_3_, ...), custom_call_target="tpu_custom_call" | custom-call | tf_op jit(solution)/shard_map/local_states/pallas_call | solution.py:122
  32.8 0.0 copy-start.3
  32.8 11.4 %state_gather.1 = f32[8,2,17,8,128]{4,3,2,1,0:T(8,128)S(1)} custom-call(f32[2,17,8,128]{3,2,1,0:T(8,128)S(1)} %pad_maximum_fusion.refs_0_), custom_call_target="tpu_custom_call" | custom-call | tf_op jit(solution)/shard_map/state_gather/pallas_call | solution.py:259
  44.3 0.2 fusion.7.refs_4_
  44.5 4.0 %gated_output.1.refs_0_ = bf16[128,1024]{1,0:T(8,128)(2,1)S(1)} custom-call(f32[1024,128]{1,0:T(8,128)S(1)} %get-tuple-element.11.refs_0_, f32[1024,128]{1,0:T(8,128)S(1)} %get-tuple-element.12.refs_1_, f32[16,8,128]{2,1,0:T(8,128)S(1)} %bitcast.96, f32[4096]{0:T(1024)S(1)} %reshape.144.refs_5_.refs_3_, f32[2,16,8,128]{3,2,1,0:T(8,128)S(1)} %fusion.7.refs_4_, ...), custom_call_target="tpu_custom_call" | custom-call | tf_op jit(solution)/shard_map/gated_output/pallas_call | solution.py:142
  48.5 0.0 copy-start.7
  48.5 51.4 %mix.1 = (f32[32,4096]{1,0:T(8,128)S(1)}, bf16[128,4096]{1,0:T(8,128)(2,1)S(1)}) custom-call(bf16[128,1024]{1,0:T(8,128)(2,1)S(1)} %gated_output.1.refs_0_, bf16[1024,4096]{1,0:T(8,128)(2,1)} %refs_1_.3, bf16[32,4096]{1,0:T(8,128)(2,1)S(1)} %reshape.148.refs_2_, bf16[1,4096]{1,0:T(2,128)(2,1)S(1)} %reshape.149.refs_3_, bf16[4,4096]{1,0:T(4,128)(2,1)S(1)} %copy-done.3, ...), custom_call_target="tpu_custom_call" | custom-call | tf_op jit(solution)/shard_map/mix/pallas_call | solution.py:607
  99.9 0.0 copy-start.1
  99.9 1.2 convolution_convert_fusion.refs_0_
  101.1 0.4 fusion.20
  101.6 0.1 multiply_reduce_fusion
  101.7 0.1 select_reduce_fusion
  101.8 0.7 copy.46.refs_5_
  102.5 69.0 %experts.1 = f32[32,4096]{1,0:T(8,128)} custom-call(bf16[80,4096]{1,0:T(8,128)(2,1)} %convolution_convert_fusion.refs_0_, bf16[4096,256]{1,0:T(8,128)(2,1)} %bitcast.100, bf16[4096,256]{1,0:T(8,128)(2,1)} %bitcast.101, bf16[256,4096]{1,0:T(8,128)(2,1)} %bitcast.102, bf16[128,80]{1,0:T(8,128)(2,1)} %fusion.15.refs_4_, f32[80,1]{1,0:T(8,128)} %copy.46.refs_5_, ...), custom_call_target="tpu_custom_call" | custom-call | tf_op jit(solution)/shard_map/experts/pallas_call | solution.py:477
  171.5 2.1 %reshape.151 = f32[16,2,4096]{2,1,0:T(2,128)} reshape(f32[32,4096]{1,0:T(8,128)} %experts.1) | data formatting | bytes 1048576 | tf_op jit(solution)/shard_map/reshape | solution.py:721
  (25 shorter events, 0.2 us)
Async XLA Ops:
  0.0 13.5 %copy-start = (bf16[1024,288]{0,1:T(8,128)(2,1)S(1)}, bf16[1024,288]{0,1:T(8,128)(2,1)}, u32[]{:S(2)}) copy-start(bf16[1024,288]{0,1:T(8,128)(2,1)} %param.26) | copy-start | bytes 1769476
  0.0 11.9 %copy-start.6 = (bf16[64,2,1024]{2,1,0:T(2,128)(2,1)S(1)}, bf16[64,2,1024]{2,1,0:T(2,128)(2,1)}, u32[]{:S(2)}) copy-start(bf16[64,2,1024]{2,1,0:T(2,128)(2,1)} %param.22) | copy-start | bytes 786436
  0.0 11.6 %copy-start.9 = (bf16[4096]{0:T(1024)(128)(2,1)S(1)}, bf16[4096]{0:T(1024)(128)(2,1)}, u32[]{:S(2)}) copy-start(bf16[4096]{0:T(1024)(128)(2,1)} %param.34) | copy-start | bytes 24580
  0.0 11.6 %copy-start.10 = (bf16[4096]{0:T(1024)(128)(2,1)S(1)}, bf16[4096]{0:T(1024)(128)(2,1)}, u32[]{:S(2)}) copy-start(bf16[4096]{0:T(1024)(128)(2,1)} %param.36) | copy-start | bytes 24580
  0.0 11.8 %copy-start.8 = (bf16[3,2,1024]{2,1,0:T(2,128)(2,1)S(1)}, bf16[3,2,1024]{2,1,0:T(2,128)(2,1)}, u32[]{:S(2)}) copy-start(bf16[3,2,1024]{2,1,0:T(2,128)(2,1)} %param.32) | copy-start | bytes 36868
  0.8 11.0 %collective-permute-start = (bf16[3,2,1024]{2,1,0:T(2,128)(2,1)S(1)}, bf16[3,2,1024]{2,1,0:T(2,128)(2,1)S(1)}, u32[]{:S(2)}, u32[]{:S(2)}) collective-permute-start(bf16[3,2,1024]{2,1,0:T(2,128)(2,1)S(1)} %slice.115), channel_id=1, source_target_pairs={{0,4},{4,8},{8,12},{12,16},{16,20},{20,24},{24,28},{1,5},{5,9},{9,... | collective-permute-start | bytes 36872 | tf_op jit(solution)/shard_map/ppermute | solution.py:16
  13.1 15.9 %copy-start.2 = (bf16[256,1024]{1,0:T(8,128)(2,1)S(1)}, bf16[256,1024]{1,0:T(8,128)(2,1)}, u32[]{:S(2)}) copy-start(bf16[256,1024]{1,0:T(8,128)(2,1)} %refs_1_.2) | copy-start | bytes 1572868
  13.1 15.9 %copy-start.4 = (f32[1024]{0:T(1024)S(1)}, f32[1024]{0:T(1024)}, u32[]{:S(2)}) copy-start(f32[1024]{0:T(1024)} %param.28) | copy-start | bytes 12292
  29.0 15.5 %copy-start.5 = (f32[1024]{0:T(1024)S(1)}, f32[1024]{0:T(1024)}, u32[]{:S(2)}) copy-start(f32[1024]{0:T(1024)} %param.30) | copy-start | bytes 12292
  32.8 15.7 %copy-start.3 = (bf16[4,4096]{1,0:T(4,128)(2,1)S(1)}, bf16[4,4096]{1,0:T(4,128)(2,1)}, u32[]{:S(2)}) copy-start(bf16[4,4096]{1,0:T(4,128)(2,1)} %refs_4_.1) | copy-start | bytes 98308
  48.5 52.6 %copy-start.7 = (bf16[4096,4]{0,1:T(4,128)(2,1)S(1)}, bf16[4096,4]{0,1:T(4,128)(2,1)}, u32[]{:S(2)}) copy-start(bf16[4096,4]{0,1:T(4,128)(2,1)} %param.37) | copy-start | bytes 98308
  99.9 1.5 copy-start.1
